TPU v7x, 128 devices: a whole 4x4x4 slice. The times are simulated.
128 devices in a mesh: pipe: 2 (over core), expert: 16 (over z, x), tensor: 4 (over y).
Axes of the slice: x: 4, y: 4, z: 4, core: 2. Of those that a mesh axis runs over, the one named last changes fastest.
Arguments:
- inputs: bfloat16 [2, 2048, 2048], P(None, 'expert'), may hold values from -6 to 6
- cotangent: bfloat16 [2, 2048, 2048], P(None, 'expert'), may hold values from -6 to 6
- doc_bounds: int32 [2, 16, 2], P(None, 'expert'), may hold values from 1 to 127, as said below
- routes: int32 [2, 2, 2048, 8], P('pipe', None, 'expert'), may hold values from 0 to 31, all different within a row; in each aligned block of 128 rows (0 to 127, 128 to 255, ..., all dimensions but the last counted through in order) at most 48 rows name the same one
- gates: float32 [2, 2, 2048, 8], P('pipe', None, 'expert'), may hold values from 0.06 to 0.25
- norm_attn: float32 [2, 2048], P('pipe'), may hold values from 0.1 to 1.9
- norm_moe: float32 [2, 2048], P('pipe'), may hold values from 0.1 to 1.9
- q_gain: float32 [2, 128], P('pipe'), may hold values from 0.1 to 1.9
- k_gain: float32 [2, 128], P('pipe'), may hold values from 0.1 to 1.9
- w_query: bfloat16 [2, 2048, 4096], P('pipe', 'expert', 'tensor'), may hold values from -0.125 to 0.125
- key_matrix: bfloat16 [2, 2048, 512], P('pipe', 'expert', 'tensor'), may hold values from -0.125 to 0.125
- value_matrix: bfloat16 [2, 2048, 512], P('pipe', 'expert', 'tensor'), may hold values from -0.125 to 0.125
- w_out: bfloat16 [2, 4096, 2048], P('pipe', 'tensor', 'expert'), may hold values from -0.5 to 0.5
- w_gate: bfloat16 [2, 32, 768, 2048], P('pipe', 'expert', 'tensor'), may hold values from -0.125 to 0.125
- w_up: bfloat16 [2, 32, 768, 2048], P('pipe', 'expert', 'tensor'), may hold values from -0.125 to 0.125
- w_down: bfloat16 [2, 32, 768, 2048], P('pipe', 'expert', 'tensor'), may hold values from -0.875 to 0.875
Outputs:
- activations: float32 [2, 2, 2048, 2048], P('pipe', None, 'expert')
- input_grads: float32 [2, 2, 2048, 2048], P('pipe', None, 'expert')
- d_norm_attn: float32 [2, 2048], P('pipe')
- d_norm_moe: float32 [2, 2048], P('pipe')
- d_q_gain: float32 [2, 128], P('pipe')
- d_k_gain: float32 [2, 128], P('pipe')
- d_query: float32 [2, 2048, 4096], P('pipe', 'expert', 'tensor')
- d_key: float32 [2, 2048, 512], P('pipe', 'expert', 'tensor')
- d_value: float32 [2, 2048, 512], P('pipe', 'expert', 'tensor')
- d_out: float32 [2, 4096, 2048], P('pipe', 'tensor', 'expert')
- d_gate_w: float32 [2, 32, 768, 2048], P('pipe', 'expert', 'tensor')
- d_up_w: float32 [2, 32, 768, 2048], P('pipe', 'expert', 'tensor')
- d_down_w: float32 [2, 32, 768, 2048], P('pipe', 'expert', 'tensor')
- d_gates: float32 [2, 2, 2048, 8], P('pipe', None, 'expert')
Inputs may be any that keep to these rules, and one draw needn't show every extreme that they name: `routes`: in each aligned block of 128 rows (one group of one layer and micro-batch) no expert is named by more than 48 rows; a row names 8 different experts. `doc_bounds`: each pair (s, e) has s < 64 < e, so that a group holds three documents.
All inputs are finite; a program needn't handle non-finite values.
Results may differ from a plain program's by a relative error of at most 0.03.
Values may be sent and summed in bfloat16 or wider, within the bound.
A program may use at most 320 MiB of HBM per device.

v0:
```python
import jax
import jax.numpy as jnp
from jax import lax
from jax.sharding import PartitionSpec as P

HEAD_SIZE = 128
TOPK = 8


eps = 1e-06
rope_base = 1000000.0


def from_behind(block, axis, distance):
    devices = range(lax.axis_size(axis))
    route = [(i - distance, i) for i in devices if i - distance in devices]
    return lax.ppermute(block, axis, route)


def rms_scale(values):
    return lax.rsqrt(jnp.mean(values * values, axis=-1, keepdims=True) + eps)


def rotary(values, cosine, sine_table):
    half_width = values.shape[-1] // 2
    lower_half = values[..., :half_width]
    upper_half = values[..., half_width:]
    return jnp.concatenate(
        [
            lower_half * cosine - upper_half * sine_table,
            upper_half * cosine + lower_half * sine_table,
        ],
        axis=-1,
    )


def rotary_back(grad_in, cosine, sine_table):
    half_width = grad_in.shape[-1] // 2
    lower_half = grad_in[..., :half_width]
    upper_half = grad_in[..., half_width:]
    return jnp.concatenate(
        [
            lower_half * cosine + upper_half * sine_table,
            upper_half * cosine - lower_half * sine_table,
        ],
        axis=-1,
    )


def rotary_tables(positions, head_width):
    freqs = rope_base ** (-(2.0 * jnp.arange(head_width // 2, dtype=jnp.float32)) / head_width)
    angles = positions[:, None] * freqs[None, :]
    return (jnp.cos(angles)[:, None, :], jnp.sin(angles)[:, None, :])


def norm_back(grad_in, values, row_scale, gain_vec):
    weighted = grad_in * gain_vec
    d_values = row_scale * weighted - values * row_scale**3 * jnp.mean(
        weighted * values, axis=-1, keepdims=True
    )
    return (d_values, grad_in * values * row_scale)


def doc_layout(bounds, rows_total):
    row_place = jnp.arange(rows_total, dtype=jnp.int32)
    doc_start = bounds[0]
    doc_end = bounds[1]
    segment_piece = (row_place >= doc_start).astype(jnp.int32) + (row_place >= doc_end).astype(
        jnp.int32
    )
    first_place = jnp.where(
        segment_piece == 0, 0, jnp.where(segment_piece == 1, doc_start, doc_end)
    )
    return (segment_piece, (row_place - first_place).astype(jnp.float32))


def slot_layout(route_rows, expert_count, capacity):
    rows_total, top_count = route_rows.shape
    onehot = (
        route_rows[:, :, None] == jnp.arange(expert_count, dtype=jnp.int32)[None, None, :]
    ).astype(jnp.int32)
    per_row = jnp.sum(onehot, axis=1, dtype=jnp.int32)
    before = jnp.cumsum(per_row, axis=0, dtype=jnp.int32) - per_row
    slot = jnp.sum(onehot * before[:, None, :], axis=2, dtype=jnp.int32)
    slot_index = route_rows * capacity + slot
    slot_owner = jnp.full((expert_count * capacity,), rows_total * top_count, jnp.int32)
    slot_owner = slot_owner.at[slot_index.reshape(-1)].set(
        jnp.arange(rows_total * top_count, dtype=jnp.int32)
    )
    return (slot_index, slot_owner)


def masked_scores(query_rotated, key_rotated, segment_piece):
    rows_total, head_count, head_width = query_rotated.shape
    kv_count = key_rotated.shape[1]
    grouped = query_rotated.reshape(rows_total, kv_count, head_count // kv_count, head_width)
    scores = jnp.einsum(
        "rkgd,skd->kgrs", grouped, key_rotated, preferred_element_type=jnp.float32
    ) * head_width ** (-0.5)
    row_place = jnp.arange(rows_total)
    allowed = (segment_piece[:, None] == segment_piece[None, :]) & (
        row_place[None, :] <= row_place[:, None]
    )
    return (jnp.where(allowed, scores, -1e30), grouped)


def fetch_weights(shards):
    return (
        lax.all_gather(shards[0], "expert", axis=0, tiled=True),
        lax.all_gather(shards[1], "expert", axis=0, tiled=True),
        lax.all_gather(shards[2], "expert", axis=0, tiled=True),
        lax.all_gather(shards[3], "expert", axis=1, tiled=True),
    )


def send_rows(slot_rows):
    return lax.all_to_all(slot_rows, "expert", split_axis=0, concat_axis=0, tiled=True)


def return_rows(block_parts):
    return lax.all_to_all(block_parts, "expert", split_axis=0, concat_axis=0, tiled=True)


def layer_forward(
    state, segment_piece, positions, route_rows, gate_rows, gain_set, attn_w, expert_w
):
    norm_attn, norm_moe, q_gain, k_gain = gain_set
    w_query, key_matrix, value_matrix, w_out = attn_w
    w_gate, w_up, w_down = expert_w
    rows_total, model_width = state.shape
    scale_in = rms_scale(state)
    normalized_input = (state * scale_in * norm_attn).astype(jnp.bfloat16)
    query_f = jnp.dot(normalized_input, w_query, preferred_element_type=jnp.float32).reshape(
        rows_total, -1, HEAD_SIZE
    )
    key_flat = jnp.dot(normalized_input, key_matrix, preferred_element_type=jnp.float32).reshape(
        rows_total, -1, HEAD_SIZE
    )
    value_b = (
        jnp.dot(normalized_input, value_matrix, preferred_element_type=jnp.float32)
        .astype(jnp.bfloat16)
        .reshape(rows_total, -1, HEAD_SIZE)
    )
    cosine, sine_table = rotary_tables(positions, HEAD_SIZE)
    q_scale = rms_scale(query_f)
    k_scale = rms_scale(key_flat)
    query_rotated = rotary(query_f * q_scale * q_gain, cosine, sine_table).astype(jnp.bfloat16)
    key_rotated = rotary(key_flat * k_scale * k_gain, cosine, sine_table).astype(jnp.bfloat16)
    scores, grouped = masked_scores(query_rotated, key_rotated, segment_piece)
    row_peak = jnp.max(scores, axis=-1, keepdims=True)
    weights = jnp.exp(scores - row_peak)
    row_total = jnp.sum(weights, axis=-1, keepdims=True)
    probs_b = (weights / row_total).astype(jnp.bfloat16)
    log_total = row_peak + jnp.log(row_total)
    mixed_output = jnp.einsum(
        "kgrs,skd->rkgd", probs_b, value_b, preferred_element_type=jnp.float32
    )
    attended = mixed_output.reshape(rows_total, -1).astype(jnp.bfloat16)
    branch = lax.psum(jnp.dot(attended, w_out, preferred_element_type=jnp.float32), "tensor")
    middle = state + branch
    scale_mid = rms_scale(middle)
    moe_in = (middle * scale_mid * norm_moe).astype(jnp.bfloat16)
    expert_count = w_gate.shape[0] * lax.axis_size("expert")
    capacity = min(rows_total, 3 * rows_total * TOPK // (2 * expert_count))
    slot_index, slot_owner = slot_layout(route_rows, expert_count, capacity)
    extended = jnp.concatenate([moe_in, jnp.zeros((1, model_width), jnp.bfloat16)], axis=0)
    outgoing = extended[slot_owner // TOPK].reshape(
        lax.axis_size("expert"), w_gate.shape[0], capacity, model_width
    )
    arrived = send_rows(outgoing)
    gate_v = jnp.einsum("secd,efd->secf", arrived, w_gate, preferred_element_type=jnp.float32)
    up_v = jnp.einsum("secd,efd->secf", arrived, w_up, preferred_element_type=jnp.float32)
    hidden = (jax.nn.silu(gate_v) * up_v).astype(jnp.bfloat16)
    partial_out = jnp.einsum(
        "secf,efd->secd", hidden, w_down, preferred_element_type=jnp.float32
    ).astype(jnp.bfloat16)
    returned = return_rows(partial_out)
    chosen = returned.reshape(-1, model_width)[slot_index]
    mixture = lax.psum(
        jnp.einsum("rk,rkd->rd", gate_rows, chosen.astype(jnp.float32)).astype(jnp.bfloat16),
        "tensor",
    ).astype(jnp.float32)
    kept_values = (
        state,
        normalized_input,
        query_f,
        key_flat,
        q_scale,
        k_scale,
        query_rotated,
        key_rotated,
        value_b,
        log_total,
        attended,
        middle,
        scale_in,
        scale_mid,
        arrived,
        gate_v,
        up_v,
        hidden,
        chosen,
        slot_index,
        slot_owner,
        segment_piece,
        cosine,
        sine_table,
    )
    return (middle + mixture, kept_values)


def layer_backward(grad_out, kept_values, gate_rows, gain_set, attn_w, expert_w):
    norm_attn, norm_moe, q_gain, k_gain = gain_set
    w_query, key_matrix, value_matrix, w_out = attn_w
    w_gate, w_up, w_down = expert_w
    (
        state,
        normalized_input,
        query_f,
        key_flat,
        q_scale,
        k_scale,
        query_rotated,
        key_rotated,
        value_b,
        log_total,
        attended,
        middle,
        scale_in,
        scale_mid,
        arrived,
        gate_v,
        up_v,
        hidden,
        chosen,
        slot_index,
        slot_owner,
        segment_piece,
        cosine,
        sine_table,
    ) = kept_values
    rows_total, model_width = state.shape
    slot_grads = (
        (gate_rows[:, :, None] * grad_out[:, None, :]).astype(jnp.bfloat16).reshape(-1, model_width)
    )
    slot_table = jnp.concatenate([slot_grads, jnp.zeros((1, model_width), jnp.bfloat16)], axis=0)
    d_part = send_rows(slot_table[slot_owner].reshape(arrived.shape))
    gate_part = jnp.einsum("rkd,rd->rk", chosen.astype(jnp.float32), grad_out)
    d_hidden = jnp.einsum("secd,efd->secf", d_part, w_down, preferred_element_type=jnp.float32)
    sigmoid_g = jax.nn.sigmoid(gate_v)
    d_gate_v = (d_hidden * up_v * sigmoid_g * (1.0 + gate_v * (1.0 - sigmoid_g))).astype(
        jnp.bfloat16
    )
    d_up_v = (d_hidden * gate_v * sigmoid_g).astype(jnp.bfloat16)
    grad_down = jnp.einsum("secf,secd->efd", hidden, d_part, preferred_element_type=jnp.float32)
    grad_gate = jnp.einsum("secf,secd->efd", d_gate_v, arrived, preferred_element_type=jnp.float32)
    grad_up = jnp.einsum("secf,secd->efd", d_up_v, arrived, preferred_element_type=jnp.float32)
    d_rows = jnp.einsum("secf,efd->secd", d_gate_v, w_gate, preferred_element_type=jnp.float32)
    d_rows = (
        d_rows + jnp.einsum("secf,efd->secd", d_up_v, w_up, preferred_element_type=jnp.float32)
    ).astype(jnp.bfloat16)
    d_back = return_rows(d_rows)
    d_moe_part = jnp.sum(d_back.reshape(-1, model_width)[slot_index].astype(jnp.float32), axis=1)
    d_moe_in, gate_grads = (
        lax.psum(d_moe_part.astype(jnp.bfloat16), "tensor").astype(jnp.float32),
        lax.psum(gate_part.astype(jnp.bfloat16), "tensor").astype(jnp.float32),
    )
    d_mid_norm, moe_gain_rows = norm_back(d_moe_in, middle, scale_mid, norm_moe)
    d_middle = grad_out + d_mid_norm
    d_branch = d_middle.astype(jnp.bfloat16)
    grad_out_w = jnp.einsum("rh,rd->hd", attended, d_branch, preferred_element_type=jnp.float32)
    kv_count = key_rotated.shape[1]
    d_att = jnp.einsum("rd,hd->rh", d_branch, w_out, preferred_element_type=jnp.float32).astype(
        jnp.bfloat16
    )
    d_att = d_att.reshape(rows_total, kv_count, -1, HEAD_SIZE)
    scores, grouped = masked_scores(query_rotated, key_rotated, segment_piece)
    prob_f = jnp.exp(scores - log_total)
    d_prob = jnp.einsum("rkgd,skd->kgrs", d_att, value_b, preferred_element_type=jnp.float32)
    d_value_b = jnp.einsum(
        "kgrs,rkgd->skd", prob_f.astype(jnp.bfloat16), d_att, preferred_element_type=jnp.float32
    ).astype(jnp.bfloat16)
    row_delta = jnp.sum(prob_f * d_prob, axis=-1, keepdims=True)
    d_scores = (prob_f * (d_prob - row_delta)).astype(jnp.bfloat16)
    score_scale = HEAD_SIZE ** (-0.5)
    d_query_r = (
        jnp.einsum(
            "kgrs,skd->rkgd", d_scores, key_rotated, preferred_element_type=jnp.float32
        ).reshape(query_rotated.shape)
        * score_scale
    )
    d_key_r = (
        jnp.einsum("kgrs,rkgd->skd", d_scores, grouped, preferred_element_type=jnp.float32)
        * score_scale
    )
    d_query_n, q_gain_rows = norm_back(
        rotary_back(d_query_r, cosine, sine_table), query_f, q_scale, q_gain
    )
    d_key_n, k_gain_rows = norm_back(
        rotary_back(d_key_r, cosine, sine_table), key_flat, k_scale, k_gain
    )
    d_query_b = d_query_n.astype(jnp.bfloat16).reshape(rows_total, -1)
    d_key_b = d_key_n.astype(jnp.bfloat16).reshape(rows_total, -1)
    d_value_flat = d_value_b.reshape(rows_total, -1)
    grad_query = jnp.einsum(
        "rd,rh->dh", normalized_input, d_query_b, preferred_element_type=jnp.float32
    )
    grad_key = jnp.einsum(
        "rd,rh->dh", normalized_input, d_key_b, preferred_element_type=jnp.float32
    )
    grad_value = jnp.einsum(
        "rd,rh->dh", normalized_input, d_value_flat, preferred_element_type=jnp.float32
    )
    d_normed = jnp.einsum("rh,dh->rd", d_query_b, w_query, preferred_element_type=jnp.float32)
    d_normed = d_normed + jnp.einsum(
        "rh,dh->rd", d_key_b, key_matrix, preferred_element_type=jnp.float32
    )
    d_normed = d_normed + jnp.einsum(
        "rh,dh->rd", d_value_flat, value_matrix, preferred_element_type=jnp.float32
    )
    d_normed = lax.psum(d_normed.astype(jnp.bfloat16), "tensor").astype(jnp.float32)
    d_state_norm, attn_gain_rows = norm_back(d_normed, state, scale_in, norm_attn)
    d_state = d_middle + d_state_norm
    grad_set = (
        jnp.sum(attn_gain_rows, axis=0),
        jnp.sum(moe_gain_rows, axis=0),
        jnp.sum(q_gain_rows, axis=(0, 1)),
        jnp.sum(k_gain_rows, axis=(0, 1)),
        grad_query,
        grad_key,
        grad_value,
        grad_out_w,
        grad_gate,
        grad_up,
        grad_down,
    )
    return (d_state, gate_grads, grad_set)


def body(
    inputs,
    cotangent,
    doc_bounds,
    routes,
    gates,
    norm_attn,
    norm_moe,
    q_gain,
    k_gain,
    w_query,
    key_matrix,
    value_matrix,
    w_out,
    w_gate,
    w_up,
    w_down,
):
    section_index = lax.axis_index("pipe")
    batch_count, rows_total, model_width = inputs.shape
    gain_set = (norm_attn[0], norm_moe[0], q_gain[0], k_gain[0])
    shards = (w_query[0], key_matrix[0], value_matrix[0], w_out[0])
    expert_w = (w_gate[0], w_up[0], w_down[0])
    route_all = routes[0]
    gate_all = gates[0]
    carried = jnp.zeros((rows_total, model_width), jnp.float32)
    activations = jnp.zeros((batch_count, rows_total, model_width), jnp.float32)
    kept_steps = []
    for step_number in range(batch_count + 1):
        offset = step_number - section_index
        batch_index = jnp.clip(offset, 0, batch_count - 1)
        active = (offset >= 0) & (offset < batch_count)
        fresh_rows = lax.dynamic_index_in_dim(inputs, batch_index, 0, keepdims=False).astype(
            jnp.float32
        )
        state = jnp.where(section_index == 0, fresh_rows, carried)
        bounds = lax.dynamic_index_in_dim(doc_bounds, batch_index, 0, keepdims=False)[0]
        segment_piece, positions = doc_layout(bounds, rows_total)
        route_rows = lax.dynamic_index_in_dim(route_all, batch_index, 0, keepdims=False)
        gate_rows = lax.dynamic_index_in_dim(gate_all, batch_index, 0, keepdims=False)
        attn_w = fetch_weights(shards)
        result, kept_values = layer_forward(
            state, segment_piece, positions, route_rows, gate_rows, gain_set, attn_w, expert_w
        )
        activations = jnp.where(
            active,
            lax.dynamic_update_index_in_dim(activations, result, batch_index, 0),
            activations,
        )
        kept_steps.append(kept_values)
        carried = from_behind(result.astype(jnp.bfloat16), "pipe", 1).astype(jnp.float32)
    carried_grad = jnp.zeros((rows_total, model_width), jnp.float32)
    input_grads = jnp.zeros((batch_count, rows_total, model_width), jnp.float32)
    gate_grad_all = jnp.zeros(gate_all.shape, jnp.float32)
    totals = None
    for step_number in range(batch_count + 1):
        offset = step_number - (1 - section_index)
        batch_index = jnp.clip(offset, 0, batch_count - 1)
        active = (offset >= 0) & (offset < batch_count)
        kept_index = jnp.clip(batch_index + section_index, 0, batch_count)
        kept_values = kept_steps[0]
        for earlier in range(1, batch_count + 1):
            kept_values = jax.tree.map(
                lambda before_v, after_v: jnp.where(kept_index == earlier, after_v, before_v),
                kept_values,
                kept_steps[earlier],
            )
        given = lax.dynamic_index_in_dim(cotangent, batch_index, 0, keepdims=False).astype(
            jnp.float32
        )
        incoming = jnp.where(section_index == 1, given, carried_grad)
        incoming = jnp.where(active, incoming, jnp.zeros_like(incoming))
        gate_rows = lax.dynamic_index_in_dim(gate_all, batch_index, 0, keepdims=False)
        attn_w = fetch_weights(shards)
        d_state, gate_grads, grad_set = layer_backward(
            incoming, kept_values, gate_rows, gain_set, attn_w, expert_w
        )
        totals = (
            grad_set
            if totals is None
            else jax.tree.map(lambda summed, added: summed + added, totals, grad_set)
        )
        input_grads = jnp.where(
            active,
            lax.dynamic_update_index_in_dim(input_grads, d_state, batch_index, 0),
            input_grads,
        )
        gate_grad_all = jnp.where(
            active,
            lax.dynamic_update_index_in_dim(gate_grad_all, gate_grads, batch_index, 0),
            gate_grad_all,
        )
        carried_grad = from_behind(d_state.astype(jnp.bfloat16), "pipe", -1).astype(jnp.float32)
    (
        attn_gain_sum,
        moe_gain_sum,
        q_gain_sum,
        k_gain_sum,
        grad_query,
        grad_key,
        grad_value,
        grad_out_w,
        grad_gate,
        grad_up,
        grad_down,
    ) = totals
    d_query, d_key, d_value, d_out = (
        lax.psum_scatter(
            grad_query.astype(jnp.bfloat16), "expert", scatter_dimension=0, tiled=True
        ).astype(jnp.float32),
        lax.psum_scatter(
            grad_key.astype(jnp.bfloat16), "expert", scatter_dimension=0, tiled=True
        ).astype(jnp.float32),
        lax.psum_scatter(
            grad_value.astype(jnp.bfloat16), "expert", scatter_dimension=0, tiled=True
        ).astype(jnp.float32),
        lax.psum_scatter(
            grad_out_w.astype(jnp.bfloat16), "expert", scatter_dimension=1, tiled=True
        ).astype(jnp.float32),
    )
    tensor_count = lax.axis_size("tensor")
    d_norm_attn, d_norm_moe, d_q_gain, d_k_gain = lax.psum(
        (attn_gain_sum / tensor_count, moe_gain_sum / tensor_count, q_gain_sum, k_gain_sum),
        ("expert", "tensor"),
    )
    return (
        activations[None],
        input_grads[None],
        d_norm_attn[None],
        d_norm_moe[None],
        d_q_gain[None],
        d_k_gain[None],
        d_query[None],
        d_key[None],
        d_value[None],
        d_out[None],
        grad_gate[None],
        grad_up[None],
        grad_down[None],
        gate_grad_all[None],
    )


def solution(mesh):
    placed = (
        P(None, "expert", None),
        P(None, "expert", None),
        P(None, "expert", None),
        P("pipe", None, "expert", None),
        P("pipe", None, "expert", None),
        P("pipe", None),
        P("pipe", None),
        P("pipe", None),
        P("pipe", None),
        P("pipe", "expert", "tensor"),
        P("pipe", "expert", "tensor"),
        P("pipe", "expert", "tensor"),
        P("pipe", "tensor", "expert"),
        P("pipe", "expert", "tensor", None),
        P("pipe", "expert", "tensor", None),
        P("pipe", "expert", "tensor", None),
    )
    return jax.shard_map(
        body,
        mesh=mesh,
        in_specs=placed,
        out_specs=(
            P("pipe", None, "expert", None),
            P("pipe", None, "expert", None),
            P("pipe", None),
            P("pipe", None),
            P("pipe", None),
            P("pipe", None),
            P("pipe", "expert", "tensor"),
            P("pipe", "expert", "tensor"),
            P("pipe", "expert", "tensor"),
            P("pipe", "tensor", "expert"),
            P("pipe", "expert", "tensor", None),
            P("pipe", "expert", "tensor", None),
            P("pipe", "expert", "tensor", None),
            P("pipe", None, "expert", None),
        ),
        check_vma=False,
    )
```

profile of v0, /device:TPU:0, one launch (start us, length us, event | category | flops | bytes accessed | tf_op | source)
XLA Modules:
  0.0 2456.2 jit_solution(11306326430564807872)
XLA Ops:
  10.1 26.1 %all-gather.1 = bf16[1,2048,128]{2,1,0:T(8,128)(2,1)S(1)} all-gather(bf16[1,128,128]{2,1,0:T(8,128)(2,1)} %param.26), channel_id=3, replica_groups=mesh['pipe'=2,'expert'=16,'tensor'=4] {'expert'}, dimensions={1}, use_global_device_ids=true | all-gather | bytes 557056 | tf_op jit(solution)/shard_map/all_gather | solution.py:110
  88.5 38.2 %all-gather.9.cloned.1.call-done = bf16[1,1024,2048]{2,1,0:T(8,128)(2,1)} async-done(((bf16[1,1024,128]{2,1,0:T(8,128)(2,1)}), bf16[1,1024,2048]{2,1,0:T(8,128)(2,1)}) %all-gather.9.cloned.1.call-update) | async-done | bytes 4194320 | tf_op jit(solution)/shard_map/all_gather | solution.py:112
  146.1 29.7 %all-reduce.21.cloned.1.call-done = f32[128,2048]{1,0:T(8,128)} async-done(((f32[128,2048]{1,0:T(8,128)}), f32[128,2048]{1,0:T(8,128)}) %all-reduce.21.cloned.1.call-update) | async-done | bytes 1048592 | tf_op jit(solution)/shard_map/psum | solution.py:159
  185.5 81.1 %all_to_all.60 = bf16[16,2,48,2048]{3,2,1,0:T(8,128)(2,1)S(1)} all-to-all(bf16[16,2,48,2048]{3,2,1,0:T(8,128)(2,1)} %bitcast.1052), channel_id=1, replica_groups=mesh['pipe'=2,'expert'=16,'tensor'=4] {'expert'}, dimensions={0} | all-to-all | bytes 12582912 | tf_op jit(solution)/shard_map/all_to_all | solution.py:117
  284.7 86.7 %all-to-all-done.1 = bf16[16,2,48,2048]{3,2,1,0:T(8,128)(2,1)} async-done(((bf16[16,2,48,2048]{3,2,1,0:T(8,128)(2,1)}), bf16[16,2,48,2048]{3,2,1,0:T(8,128)(2,1)}, u32[]{:S(2)}, u32[]{:S(2)}) %all-to-all-start.1) | async-done | bytes 6291488 | tf_op jit(solution)/shard_map/all_to_all | solution.py:121
  388.4 42.7 %all-reduce.23.cloned.1.call-done = bf16[128,2048]{1,0:T(8,128)(2,1)} async-done(((bf16[128,2048]{1,0:T(8,128)(2,1)}), bf16[128,2048]{1,0:T(8,128)(2,1)}) %all-reduce.23.cloned.1.call-update) | async-done | bytes 524304 | tf_op jit(solution)/shard_map/psum | solution.py:179
  448.5 46.6 %all-reduce.25.cloned.1.call-done = f32[128,2048]{1,0:T(8,128)} async-done(((f32[128,2048]{1,0:T(8,128)}), f32[128,2048]{1,0:T(8,128)}) %all-reduce.25.cloned.1.call-update) | async-done | bytes 1048592 | tf_op jit(solution)/shard_map/psum | solution.py:159
  504.9 80.9 %all_to_all.61 = bf16[16,2,48,2048]{3,2,1,0:T(8,128)(2,1)S(1)} all-to-all(bf16[16,2,48,2048]{3,2,1,0:T(8,128)(2,1)} %bitcast.1053), channel_id=1, replica_groups=mesh['pipe'=2,'expert'=16,'tensor'=4] {'expert'}, dimensions={0} | all-to-all | bytes 12582912 | tf_op jit(solution)/shard_map/all_to_all | solution.py:117
  602.7 87.9 %all-to-all-done.3 = bf16[16,2,48,2048]{3,2,1,0:T(8,128)(2,1)} async-done(((bf16[16,2,48,2048]{3,2,1,0:T(8,128)(2,1)}), bf16[16,2,48,2048]{3,2,1,0:T(8,128)(2,1)}, u32[]{:S(2)}, u32[]{:S(2)}) %all-to-all-start.3) | async-done | bytes 6291488 | tf_op jit(solution)/shard_map/all_to_all | solution.py:121
  707.6 42.7 %all-reduce.27.cloned.1.call-done = bf16[128,2048]{1,0:T(8,128)(2,1)} async-done(((bf16[128,2048]{1,0:T(8,128)(2,1)}), bf16[128,2048]{1,0:T(8,128)(2,1)}) %all-reduce.27.cloned.1.call-update) | async-done | bytes 524304 | tf_op jit(solution)/shard_map/psum | solution.py:179
  774.8 46.5 %all-reduce.29.cloned.1.call-done = f32[128,2048]{1,0:T(8,128)} async-done(((f32[128,2048]{1,0:T(8,128)}), f32[128,2048]{1,0:T(8,128)}) %all-reduce.29.cloned.1.call-update) | async-done | bytes 1048592 | tf_op jit(solution)/shard_map/psum | solution.py:159
  858.8 69.9 %all-to-all-done.4 = bf16[16,2,48,2048]{3,2,1,0:T(8,128)(2,1)} async-done(((bf16[16,2,48,2048]{3,2,1,0:T(8,128)(2,1)}), bf16[16,2,48,2048]{3,2,1,0:T(8,128)(2,1)}, u32[]{:S(2)}, u32[]{:S(2)}) %all-to-all-start.4) | async-done | bytes 6291488 | tf_op jit(solution)/shard_map/all_to_all | solution.py:117
  946.2 75.8 %all-to-all-done.6 = bf16[16,2,48,2048]{3,2,1,0:T(8,128)(2,1)} async-done(((bf16[16,2,48,2048]{3,2,1,0:T(8,128)(2,1)}), bf16[16,2,48,2048]{3,2,1,0:T(8,128)(2,1)}, u32[]{:S(2)}, u32[]{:S(2)}) %all-to-all-start.6) | async-done | bytes 6291488 | tf_op jit(solution)/shard_map/all_to_all | solution.py:117
  1050.5 82.9 %all-to-all-done.7 = bf16[16,2,48,2048]{3,2,1,0:T(8,128)(2,1)} async-done(((bf16[16,2,48,2048]{3,2,1,0:T(8,128)(2,1)}), bf16[16,2,48,2048]{3,2,1,0:T(8,128)(2,1)}, u32[]{:S(2)}, u32[]{:S(2)}) %all-to-all-start.7) | async-done | bytes 6291488 | tf_op jit(solution)/shard_map/all_to_all | solution.py:121
  1157.0 38.7 %all-reduce.31.cloned.1.call-done = bf16[128,2048]{1,0:T(8,128)(2,1)} async-done(((bf16[128,2048]{1,0:T(8,128)(2,1)}), bf16[128,2048]{1,0:T(8,128)(2,1)}) %all-reduce.31.cloned.1.call-update) | async-done | bytes 524304 | tf_op jit(solution)/shard_map/psum | solution.py:265
  1216.6 43.8 %all-reduce.33.cloned.1.call-done = bf16[128,2048]{1,0:T(8,128)(2,1)} async-done(((bf16[128,2048]{1,0:T(8,128)(2,1)}), bf16[128,2048]{1,0:T(8,128)(2,1)}) %all-reduce.33.cloned.1.call-update) | async-done | bytes 524304 | tf_op jit(solution)/shard_map/psum | solution.py:321
  1291.5 81.0 %all_to_all.62 = bf16[16,2,48,2048]{3,2,1,0:T(8,128)(2,1)S(1)} all-to-all(bf16[16,2,48,2048]{3,2,1,0:T(8,128)(2,1)} %bitcast.1054), channel_id=1, replica_groups=mesh['pipe'=2,'expert'=16,'tensor'=4] {'expert'}, dimensions={0} | all-to-all | bytes 12582912 | tf_op jit(solution)/shard_map/all_to_all | solution.py:117
  1395.8 91.7 %all-to-all-done.9 = bf16[16,2,48,2048]{3,2,1,0:T(8,128)(2,1)} async-done(((bf16[16,2,48,2048]{3,2,1,0:T(8,128)(2,1)}), bf16[16,2,48,2048]{3,2,1,0:T(8,128)(2,1)}, u32[]{:S(2)}, u32[]{:S(2)}) %all-to-all-start.9) | async-done | bytes 6291488 | tf_op jit(solution)/shard_map/all_to_all | solution.py:121
  1508.4 39.2 %all-reduce.35.cloned.1.call-done = bf16[128,2048]{1,0:T(8,128)(2,1)} async-done(((bf16[128,2048]{1,0:T(8,128)(2,1)}), bf16[128,2048]{1,0:T(8,128)(2,1)}) %all-reduce.35.cloned.1.call-update) | async-done | bytes 524304 | tf_op jit(solution)/shard_map/psum | solution.py:265
  1568.8 43.8 %all-reduce.37.cloned.1.call-done = bf16[128,2048]{1,0:T(8,128)(2,1)} async-done(((bf16[128,2048]{1,0:T(8,128)(2,1)}), bf16[128,2048]{1,0:T(8,128)(2,1)}) %all-reduce.37.cloned.1.call-update) | async-done | bytes 524304 | tf_op jit(solution)/shard_map/psum | solution.py:321
  1642.8 81.0 %all_to_all.63 = bf16[16,2,48,2048]{3,2,1,0:T(8,128)(2,1)S(1)} all-to-all(bf16[16,2,48,2048]{3,2,1,0:T(8,128)(2,1)} %bitcast.1055), channel_id=1, replica_groups=mesh['pipe'=2,'expert'=16,'tensor'=4] {'expert'}, dimensions={0} | all-to-all | bytes 12582912 | tf_op jit(solution)/shard_map/all_to_all | solution.py:117
  1752.9 85.8 %all-to-all-done.11 = bf16[16,2,48,2048]{3,2,1,0:T(8,128)(2,1)} async-done(((bf16[16,2,48,2048]{3,2,1,0:T(8,128)(2,1)}), bf16[16,2,48,2048]{3,2,1,0:T(8,128)(2,1)}, u32[]{:S(2)}, u32[]{:S(2)}) %all-to-all-start.11) | async-done | bytes 6291488 | tf_op jit(solution)/shard_map/all_to_all | solution.py:121
  1884.1 48.5 %all-to-all-done.5 = bf16[16,2,48,2048]{3,2,1,0:T(8,128)(2,1)} async-done(((bf16[16,2,48,2048]{3,2,1,0:T(8,128)(2,1)}), bf16[16,2,48,2048]{3,2,1,0:T(8,128)(2,1)}, u32[]{:S(2)}, u32[]{:S(2)}) %all-to-all-start.5) | async-done | bytes 6291488 | tf_op jit(solution)/shard_map/all_to_all | solution.py:121
  2093.5 343.7 %all-reduce.6 = (f32[1,2048]{1,0:T(1,128)}, f32[1,2048]{1,0:T(1,128)}, f32[1,128]{1,0:T(1,128)}, f32[1,128]{1,0:T(1,128)}) all-reduce(f32[1,2048]{1,0:T(1,128)S(1)} %bitcast.1134, f32[1,2048]{1,0:T(1,128)S(1)} %bitcast.1133, ...), channel_id=1, replica_groups=mesh['pipe'=2,'expert'=16,'tensor'=4] {'expert','tensor'}, use_global_device_ids=true, to_apply=%region_63.64 | all-reduce | flops 4352 | bytes 34816 | tf_op jit(solution)/shard_map/psum | solution.py:461
  (1035 shorter events, 702.5 us)
Async XLA Ops:
  8.0 118.7 %all-gather.9.cloned.1.call-start = ((), (), s32[]{:S(2)}) async-start(), calls=%async_computation.30 | async-start | bytes 4456448 | tf_op jit(solution)/shard_map/all_gather | solution.py:112
  8.7 167.1 %all-reduce.21.cloned.1.call-start = ((), (), s32[]{:S(2)}) async-start(), calls=%async_computation.16 | async-start | bytes 2097152 | tf_op jit(solution)/shard_map/psum | solution.py:159
  278.3 93.1 %all-to-all-start.1 = ((bf16[16,2,48,2048]{3,2,1,0:T(8,128)(2,1)}), bf16[16,2,48,2048]{3,2,1,0:T(8,128)(2,1)}, u32[]{:S(2)}, u32[]{:S(2)}) async-start(bf16[16,2,48,2048]{3,2,1,0:T(8,128)(2,1)} %copy.255), calls=%async_computation.1 | async-start | bytes 12582912 | tf_op jit(solution)/shard_map/all_to_all | solution.py:121
  283.1 148.1 %all-reduce.23.cloned.1.call-start = ((), (), s32[]{:S(2)}) async-start(), calls=%async_computation.17 | async-start | bytes 1048576 | tf_op jit(solution)/shard_map/psum | solution.py:179
  388.3 106.8 %all-reduce.25.cloned.1.call-start = ((), (), s32[]{:S(2)}) async-start(), calls=%async_computation.18 | async-start | bytes 2097152 | tf_op jit(solution)/shard_map/psum | solution.py:159
  597.5 93.1 %all-to-all-start.3 = ((bf16[16,2,48,2048]{3,2,1,0:T(8,128)(2,1)}), bf16[16,2,48,2048]{3,2,1,0:T(8,128)(2,1)}, u32[]{:S(2)}, u32[]{:S(2)}) async-start(bf16[16,2,48,2048]{3,2,1,0:T(8,128)(2,1)} %copy.269), calls=%async_computation.3 | async-start | bytes 12582912 | tf_op jit(solution)/shard_map/all_to_all | solution.py:121
  602.3 148.1 %all-reduce.27.cloned.1.call-start = ((), (), s32[]{:S(2)}) async-start(), calls=%async_computation.19 | async-start | bytes 1048576 | tf_op jit(solution)/shard_map/psum | solution.py:179
  707.6 113.6 %all-reduce.29.cloned.1.call-start = ((), (), s32[]{:S(2)}) async-start(), calls=%async_computation.20 | async-start | bytes 2097152 | tf_op jit(solution)/shard_map/psum | solution.py:159
  831.0 97.8 %all-to-all-start.4 = ((bf16[16,2,48,2048]{3,2,1,0:T(8,128)(2,1)}), bf16[16,2,48,2048]{3,2,1,0:T(8,128)(2,1)}, u32[]{:S(2)}, u32[]{:S(2)}) async-start(bf16[16,2,48,2048]{3,2,1,0:T(8,128)(2,1)} %bitcast.1050), calls=%async_computation.4 | async-start | bytes 12582912 | tf_op jit(solution)/shard_map/all_to_all | solution.py:117
  928.8 93.2 %all-to-all-start.6 = ((bf16[16,2,48,2048]{3,2,1,0:T(8,128)(2,1)}), bf16[16,2,48,2048]{3,2,1,0:T(8,128)(2,1)}, u32[]{:S(2)}, u32[]{:S(2)}) async-start(bf16[16,2,48,2048]{3,2,1,0:T(8,128)(2,1)} %bitcast.1051), calls=%async_computation.6 | async-start | bytes 12582912 | tf_op jit(solution)/shard_map/all_to_all | solution.py:117
  1044.2 89.2 %all-to-all-start.7 = ((bf16[16,2,48,2048]{3,2,1,0:T(8,128)(2,1)}), bf16[16,2,48,2048]{3,2,1,0:T(8,128)(2,1)}, u32[]{:S(2)}, u32[]{:S(2)}) async-start(bf16[16,2,48,2048]{3,2,1,0:T(8,128)(2,1)} %copy.287), calls=%async_computation.7 | async-start | bytes 12582912 | tf_op jit(solution)/shard_map/all_to_all | solution.py:121
  1049.5 146.2 %all-reduce.31.cloned.1.call-start = ((), (), s32[]{:S(2)}) async-start(), calls=%async_computation.21 | async-start | bytes 1048576 | tf_op jit(solution)/shard_map/psum | solution.py:265
  1151.9 108.5 %all-reduce.33.cloned.1.call-start = ((), (), s32[]{:S(2)}) async-start(), calls=%async_computation.22 | async-start | bytes 1048576 | tf_op jit(solution)/shard_map/psum | solution.py:321
  1390.8 96.8 %all-to-all-start.9 = ((bf16[16,2,48,2048]{3,2,1,0:T(8,128)(2,1)}), bf16[16,2,48,2048]{3,2,1,0:T(8,128)(2,1)}, u32[]{:S(2)}, u32[]{:S(2)}) async-start(bf16[16,2,48,2048]{3,2,1,0:T(8,128)(2,1)} %copy.301), calls=%async_computation.9 | async-start | bytes 12582912 | tf_op jit(solution)/shard_map/all_to_all | solution.py:121
  1395.6 152.0 %all-reduce.35.cloned.1.call-start = ((), (), s32[]{:S(2)}) async-start(), calls=%async_computation.23 | async-start | bytes 1048576 | tf_op jit(solution)/shard_map/psum | solution.py:265
  1505.9 106.6 %all-reduce.37.cloned.1.call-start = ((), (), s32[]{:S(2)}) async-start(), calls=%async_computation.24 | async-start | bytes 1048576 | tf_op jit(solution)/shard_map/psum | solution.py:321
  1742.1 96.6 %all-to-all-start.11 = ((bf16[16,2,48,2048]{3,2,1,0:T(8,128)(2,1)}), bf16[16,2,48,2048]{3,2,1,0:T(8,128)(2,1)}, u32[]{:S(2)}, u32[]{:S(2)}) async-start(bf16[16,2,48,2048]{3,2,1,0:T(8,128)(2,1)} %copy.315), calls=%async_computation.11 | async-start | bytes 12582912 | tf_op jit(solution)/shard_map/all_to_all | solution.py:121
  1838.7 93.9 %all-to-all-start.5 = ((bf16[16,2,48,2048]{3,2,1,0:T(8,128)(2,1)}), bf16[16,2,48,2048]{3,2,1,0:T(8,128)(2,1)}, u32[]{:S(2)}, u32[]{:S(2)}) async-start(bf16[16,2,48,2048]{3,2,1,0:T(8,128)(2,1)} %copy.283), calls=%async_computation.5 | async-start | bytes 12582912 | tf_op jit(solution)/shard_map/all_to_all | solution.py:121
  1843.6 106.0 %all-reduce.39.cloned.1.call-start = ((), (), s32[]{:S(2)}) async-start(), calls=%async_computation.25 | async-start | bytes 1048576 | tf_op jit(solution)/shard_map/psum | solution.py:265
  1869.5 221.3 %all-reduce.41.cloned.1.call-start = ((), (), s32[]{:S(2)}) async-start(), calls=%async_computation.32 | async-start | bytes 2097152 | tf_op jit(solution)/shard_map/psum | solution.py:179
  1968.6 468.6 %reduce-scatter.11.cloned.1.call-start = ((), (), s32[]{:S(2)}) async-start(), calls=%async_computation.28 | async-start | bytes 557056 | tf_op jit(solution)/shard_map/reduce_scatter | solution.py:453
  1974.0 464.6 %reduce-scatter.9.cloned.1.call-start = ((), (), s32[]{:S(2)}) async-start(), calls=%async_computation.27 | async-start | bytes 557056 | tf_op jit(solution)/shard_map/reduce_scatter | solution.py:450
  1980.3 465.2 %reduce-scatter.13.cloned.1.call-start = ((), (), s32[]{:S(2)}) async-start(), calls=%async_computation.31 | async-start | bytes 4456448
  1995.2 452.3 %reduce-scatter.7.cloned.1.call-start = ((), (), s32[]{:S(2)}) async-start(), calls=%async_computation.26 | async-start | bytes 4456448 | tf_op jit(solution)/shard_map/reduce_scatter | solution.py:447
  (319 other events, 5934.2 us)
Sparse Core Ops, SparseCore 0:
  10.2 56.9 all-gather.6
  69.4 57.2 all-gather.8
  130.7 45.0 all-reduce.20
  388.5 42.6 all-reduce.22
  448.6 46.4 all-reduce.24
  707.7 42.6 all-reduce.26
  774.9 46.3 all-reduce.28
  1152.0 43.6 all-reduce.30
  1216.7 43.6 all-reduce.32
  1506.1 41.4 all-reduce.34
  1568.9 43.6 all-reduce.36
  1869.6 43.7 all-reduce.38
  1968.8 44.8 all-reduce.40
  2016.7 73.2 reduce-scatter.10
  2093.3 71.6 reduce-scatter.8
  2168.3 76.9 reduce-scatter.12
  2248.9 76.9 reduce-scatter.6
where the time goes:
time: 2470 us; the launch traced here: 2460 us
  waiting for transfers between devices  1050 us (43%)
  blocking collectives  727 us (29%)
  local copies, waits for them, and re-layouts  249 us (10%)
  matrix products  228 us (9%)
  other arithmetic  135 us (5%)
  starting transfers between devices  49.4 us (2%)
    all_to_all x6, waiting for transfers between devices, return_rows(): lax.all_to_all(block_parts, 'expert', split_axis=0, concat_axis=0, tiled=...  484 us
    psum x1, blocking collectives, body(): lax.psum((attn_gain_sum / tensor_count, moe_gain_sum / tensor_count, q_ga...  344 us
    all_to_all x4, blocking collectives, send_rows(): lax.all_to_all(slot_rows, 'expert', split_axis=0, concat_axis=0, tiled=True)  324 us
    all_to_all x2, waiting for transfers between devices, send_rows(): lax.all_to_all(slot_rows, 'expert', split_axis=0, concat_axis=0, tiled=True)  146 us
    psum x3, waiting for transfers between devices, layer_forward(): lax.psum(jnp.dot(attended, w_out, preferred_element_type=jnp.float32), 't...  123 us
    psum x2, waiting for transfers between devices, layer_backward(): lax.psum(d_normed.astype(jnp.bfloat16), 'tensor').astype(jnp.float32)  87.6 us
    psum x3, waiting for transfers between devices, layer_forward(): lax.psum(jnp.einsum('rk,rkd->rd', gate_rows, chosen.astype(jnp.float32))....  85.5 us
    psum x3, waiting for transfers between devices, layer_backward(): lax.psum(d_moe_part.astype(jnp.bfloat16), 'tensor').astype(jnp.float32)  77.8 us
  transfers between devices with their start and end apart: 29, of which 22 were waited for; matrix products, arithmetic and copies ran while one was open for 11% of the time, Pallas kernels for 0%

commit v1 on v0

v1 whole, which is shorter than its diff:
```python
import functools
import math

import jax
import jax.numpy as jnp
from jax import lax
from jax.experimental import pallas as pl
from jax.experimental.pallas import tpu as pltpu
from jax.sharding import PartitionSpec as P

MESH = pl.DeviceIdType.MESH
ANY = pl.ANY
VM = pltpu.VMEM
F32 = jnp.float32
BF = jnp.bfloat16

HEAD_SIZE = 128
TOPK = 8
RING = 4
ROWS = 128
OWN = 32
WIDTH = 2048
HIDDEN = 384
QKV = 1280
ATT = 2304
EXPERTS = 32
GAIN_ROWS = 40
eps = 1e-06
rope_base = 1000000.0

ORDERS = (("y", "x", "z"), ("x", "z", "y"), ("z", "y", "x"))
CUTS = (
    ((0, 768), (768, 640), (1408, 640)),
    ((0, 640), (640, 768), (1408, 640)),
)
WORDERS = (("x", "z"), ("z", "x"))
WCUTS = ((0, 1152), (1152, 1152))


class Tile:
    def __init__(self, r0, rows, c0, cols, by_rows):
        self.r0, self.rows, self.c0, self.cols, self.by_rows = r0, rows, c0, cols, by_rows
        if by_rows:
            first = rows // 2
            self.spans = {
                None: (0, rows, 0, cols),
                0: (0, first, 0, cols),
                1: (first, rows - first, 0, cols),
            }
        else:
            first = (cols // 128 + 1) // 2 * 128
            self.spans = {
                None: (0, rows, 0, cols),
                0: (0, rows, 0, first),
                1: (0, rows, first, cols - first),
            }

    def shape(self, half=None):
        _, rows, _, cols = self.spans[half]
        return (rows, cols)

    def at(self, half=None):
        r, rows, c, cols = self.spans[half]
        return (pl.ds(self.r0 + r, rows), pl.ds(self.c0 + c, cols))

    def own(self):
        return Tile(0, self.rows, 0, self.cols, self.by_rows)


class Place:
    def __init__(self):
        self.pipe = lax.axis_index("pipe")
        expert = lax.axis_index("expert")
        self.at = {
            "z": lax.div(expert, RING),
            "x": lax.rem(expert, RING),
            "y": lax.axis_index("tensor"),
        }

    def step(self, axis, by):
        return lax.rem(self.at[axis] + (by + RING), RING)

    def device(self, axis, by):
        at = dict(self.at)
        at[axis] = self.step(axis, by)
        return (self.pipe, at["z"] * RING + at["x"], at["y"])

    def sibling(self):
        return (1 - self.pipe, self.at["z"] * RING + self.at["x"], self.at["y"])


class Net:
    def __init__(self, send, recv, base=0):
        self.send, self.recv, self.base, self.made = send, recv, base, []

    def describe(self, src, dst, device, i):
        return pltpu.make_async_remote_copy(
            src_ref=src,
            dst_ref=dst,
            send_sem=self.send.at[self.base + i],
            recv_sem=self.recv.at[self.base + i],
            device_id=device,
            device_id_type=MESH,
        )

    def copy(self, src, dst, device):
        made = self.describe(src, dst, device, len(self.made))
        made.start()
        self.made.append(made)
        return made

    def finish(self):
        for made in self.made:
            made.wait_send()


def greet(devices, before_wait=None):
    barrier = pltpu.get_barrier_semaphore()
    for device in devices:
        pl.semaphore_signal(barrier, inc=1, device_id=device, device_id_type=MESH)
    wait_loads()
    if before_wait is not None:
        before_wait()
    pl.semaphore_wait(barrier, len(devices))


def greet_sibling(place, devices, before_wait):
    barrier = pltpu.get_barrier_semaphore()
    for device in devices:
        pl.semaphore_signal(barrier, inc=1, device_id=device, device_id_type=MESH)

    @pl.when(place.pipe == 0)
    def _():
        pl.semaphore_signal(barrier, inc=1, device_id=place.sibling(), device_id_type=MESH)

    wait_loads()
    before_wait()

    @pl.when(place.pipe == 0)
    def _():
        pl.semaphore_wait(barrier, len(devices))

    @pl.when(place.pipe == 1)
    def _():
        pl.semaphore_wait(barrier, len(devices) + 1)


def around(place, axes):
    return [place.device(axis, by) for axis in axes for by in (1, -1)]


def together(steps):
    for _ in in_turn(steps):
        pass


def in_turn(steps):
    live = list(steps)
    while live:
        kept = []
        for step in live:
            try:
                next(step)
                kept.append(step)
            except StopIteration:
                pass
        live = kept
        if live:
            yield


def gather_ring(net, place, axis, block, first=None, seen=None):
    me, left, right, far = (place.step(axis, by) for by in (0, -1, 1, 2))
    mine = block(me, None) if first is None else first
    to_right = net.copy(mine, block(me, None), place.device(axis, 1))
    to_left = net.copy(mine, block(me, None), place.device(axis, -1))
    yield
    to_right.wait_recv()
    on_right = net.copy(block(left, 0), block(left, 0), place.device(axis, 1))
    to_left.wait_recv()
    on_left = net.copy(block(right, 1), block(right, 1), place.device(axis, -1))
    if seen is not None:
        seen(left)
        seen(right)
    yield
    on_right.wait_recv()
    on_left.wait_recv()
    if seen is not None:
        seen(far)


def gather_all(net, place, order, block, first):
    wanted = {axis: place.at[axis] for axis in order}
    for number, axis in enumerate(order):
        held = dict(wanted)

        def part(i, half, held=held, axis=axis):
            return block({**held, axis: i}, half)

        yield from gather_ring(net, place, axis, part, first if number == 0 else None)
        wanted[axis] = None


SUBS = [(chunk, sub) for chunk in range(3) for sub in range(2)]
TILES = {
    (chunk, sub): Tile(sub * 16, 16, *CUTS[sub][chunk], False) for chunk, sub in SUBS
}
TALLY_TILE = Tile(0, OWN, 0, 128, True)
STATE_TILES = [Tile(lo, 16, 0, WIDTH, False) for lo in (0, 16)]
WSUBS = [(chunk, sub) for chunk in range(2) for sub in range(2)]
WTILES = {
    (chunk, sub): Tile(sub * 64, 64, WCUTS[chunk][0], WCUTS[chunk][1], True)
    for chunk, sub in WSUBS
}


def add_into(out, terms, shape):
    def tile(spot):
        summed = terms[0][spot]
        for term in terms[1:]:
            summed = summed + term[spot]
        out[spot] = summed

    lead, rows = shape[:-2], shape[-2]
    if len(lead) == 2:

        def each(i, _):
            tile((i, slice(None), slice(None), slice(None)))
            return 0

        lax.fori_loop(0, lead[0], each, 0)
    elif rows <= OWN:
        tile((slice(None),) * len(shape))
    else:
        tiles = rows // OWN

        def each(i, _):
            spot = (pl.ds(pl.multiple_of(lax.rem(i, tiles) * OWN, OWN), OWN), slice(None))
            tile((lax.div(i, tiles),) * len(lead) + spot)
            return 0

        lax.fori_loop(0, tiles * (lead[0] if lead else 1), each, 0)


def ring_scratch(lead, tile):
    return [
        VM(lead + tile.shape(0), BF),
        VM(lead + tile.shape(1), BF),
        VM(lead + tile.shape(), BF),
        VM(lead + tile.shape(), BF),
    ]


def reduce_ring(net, place, axis, block, lead, tile, bufs, make=None):
    near_left, near_right, from_left, from_right = bufs
    whole = (slice(None),) * len(lead)

    def half_of(ref, half):
        return ref.at[whole + tile.own().at(half)]

    me, left, right, far = (place.step(axis, by) for by in (0, -1, 1, 2))
    go_right, go_left = place.device(axis, 1), place.device(axis, -1)
    if make is not None:
        make(2)
    far_right = net.copy(block(far, 0), near_left, go_right)
    far_left = net.copy(block(far, 1), near_right, go_left)
    if make is not None:
        yield
        make(1)
    own_right = net.copy(block(right, 1), half_of(from_left, 1), go_right)
    if make is not None:
        make(-1)
    own_left = net.copy(block(left, 0), half_of(from_right, 0), go_left)
    yield
    far_right.wait_recv()
    add_into(near_left, [near_left, block(right, 0)], lead + tile.shape(0))
    sum_right = net.copy(near_left, half_of(from_left, 0), go_right)
    far_left.wait_recv()
    add_into(near_right, [near_right, block(left, 1)], lead + tile.shape(1))
    sum_left = net.copy(near_right, half_of(from_right, 1), go_left)
    yield
    if make is not None:
        make(0)
    for made in (own_right, sum_right, own_left, sum_left):
        made.wait_recv()
    add_into(from_left, [from_left, block(me, None), from_right], lead + tile.shape())


def reduce_all(net, place, order, names, source, tile, bufs, make=None):
    left = [name for name in names]
    for number, axis in enumerate(order):
        spot = left.index(axis)
        lead = tuple(RING for _ in left[1:])
        if number == 0:
            block = lambda i, half, axis=axis: source({axis: i}, half)
        else:
            prior = bufs[number - 1][2]

            def block(i, half, prior=prior, spot=spot, count=len(left)):
                where = [slice(None)] * count
                where[spot] = i
                return prior.at[tuple(where) + tile.own().at(half)]

        yield from reduce_ring(
            net, place, axis, block, lead, tile, bufs[number], make if number == 0 else None
        )
        left.remove(axis)


def reduce_scratch(order_count, tile):
    return [
        ring_scratch((RING,) * (order_count - 1 - number), tile) for number in range(order_count)
    ]


def take(refs, structure):
    return [take(refs, part) if isinstance(part, list) else refs.pop(0) for part in structure]


def flat(structure):
    return [leaf for part in structure for leaf in (flat(part) if isinstance(part, list) else [part])]


def token_block(ref, tile):
    def block(wanted, half):
        where = tuple(slice(None) if wanted.get(a) is None else wanted[a] for a in ("z", "x", "y"))
        return ref.at[where + tile.at(half)]

    return block


def gather_tokens(net, place, stream, own, out):
    return in_turn(
        [
            gather_all(
                net,
                place,
                ORDERS[chunk],
                token_block(out, TILES[chunk, stream]),
                own.at[TILES[chunk, stream].at()],
            )
            for chunk in range(3)
        ]
    )


def inv_rms(values):
    return lax.rsqrt(jnp.mean(values * values, axis=-1, keepdims=True) + eps)


def tensor_blocks(ref, tile):
    def block(i, half):
        return ref.at[(i,) + tile.at(half)]

    return block


def reduce_tensor(net, place, stream, part, bufs):
    tile = STATE_TILES[stream]
    return reduce_ring(net, place, "y", tensor_blocks(part, tile), (), tile, bufs[stream])


def gather_tensor(net, place, stream, held):
    return gather_ring(net, place, "y", tensor_blocks(held, STATE_TILES[stream]))


def state_scratch():
    return flat([ring_scratch((), tile) for tile in STATE_TILES])


def state_bufs(refs):
    return take(list(refs), [[None] * 4, [None] * 4])


def norm_back(dy, values, gain):
    scale = inv_rms(values)
    weighted = dy * gain
    back = scale * weighted - values * (scale * scale * scale) * jnp.mean(
        weighted * values, axis=-1, keepdims=True
    )
    return back, dy * values * scale


TOKENS_ALL = (RING, RING, RING, OWN, WIDTH)
GATHER_COPIES = 4 * 9 * 2
REDUCE_COPIES = 6 * 9 * 2


class Load:
    def __init__(self, shape=None, pick=None):
        self.shape, self.pick = shape, pick or (lambda ref: ref)


LOAD = Load()
LOADING = []


def wait_loads():
    while LOADING:
        LOADING.pop().wait()


def loading(kernel, kinds, args):
    loads = [i for i, kind in enumerate(kinds) if isinstance(kind, Load)]
    scratch = [VM(kinds[i].shape or args[i].shape, args[i].dtype) for i in loads]
    scratch.append(pltpu.SemaphoreType.DMA((len(loads),)))

    def wrapped(*refs):
        refs, held, sems = list(refs[: -len(loads) - 1]), refs[-len(loads) - 1 : -1], refs[-1]
        for k, i in enumerate(loads):
            made = pltpu.make_async_copy(kinds[i].pick(refs[i]), held[k], sems.at[k])
            made.start()
            LOADING.append(made)
            refs[i] = held[k]
        kernel(*refs)

    return wrapped, scratch, [ANY if isinstance(kind, Load) else kind for kind in kinds]


def call(kernel, ident, shapes, in_kinds, out_kinds, scratch, args, copies, vmem=60):
    kernel, held, in_kinds = loading(kernel, in_kinds, args)
    return pl.pallas_call(
        kernel,
        out_shape=shapes,
        in_specs=[pl.BlockSpec(memory_space=kind) for kind in in_kinds],
        out_specs=[pl.BlockSpec(memory_space=kind) for kind in out_kinds],
        scratch_shapes=scratch
        + [pltpu.SemaphoreType.DMA((copies,)), pltpu.SemaphoreType.DMA((copies,))]
        + held,
        compiler_params=pltpu.CompilerParams(
            collective_id=ident, has_side_effects=True, vmem_limit_bytes=vmem * 2**20
        ),
    )(*args)


def of_pipe(ref):
    return ref.at[lax.axis_index("pipe")]


def with_sem(kernel):
    def inner(*refs):
        return kernel(*refs[:-3], refs[-2], refs[-1], refs[-3])

    return inner


def reduce_tokens(net, place, stream, part, bufs, make):
    return in_turn(
        [
            reduce_all(
                net,
                place,
                ORDERS[chunk][::-1],
                ("z", "x", "y"),
                token_block(part, TILES[chunk, stream]),
                TILES[chunk, stream],
                bufs[chunk, stream],
                functools.partial(make, chunk, stream),
            )
            for chunk in range(3)
        ]
    )


def token_scratch():
    return flat([reduce_scratch(3, TILES[sub]) for sub in SUBS])


def token_bufs(refs):
    return {sub: [[refs.pop(0) for _ in range(4)] for _ in range(3)] for sub in SUBS}


def token_sums(bufs, sub):
    return jnp.concatenate(
        [bufs[chunk, sub][-1][2][...].astype(F32) for chunk in range(3)], axis=-1
    )


def add_rows(out, rows):
    out[...] = out[...] + jnp.sum(rows, axis=0, keepdims=True)


def state_back(place, stream, base, dmid, gain, bufs, dgain, put):
    t = place.at["y"]
    rs = pl.ds(stream * 16, 16)
    summed = bufs[stream][2][...].astype(F32)
    back, rows = norm_back(summed, base[t, rs, :].astype(F32), gain[...])
    put(t, rs, (dmid[rs, :] + back).astype(BF))
    add_rows(dgain, rows)


def run_schedule(schedule, steps):
    for name in schedule:
        next(steps[name], None)
    together(steps.values())


DENSE_COPIES = 16
RING_COPIES = 32
PASS_COPIES = 28


def write_tables(bounds, pipe, cosine, sine, bias):
    start, end = bounds[pipe, 0, 0], bounds[pipe, 0, 1]
    row = lax.broadcasted_iota(jnp.int32, (ROWS, 128), 0)
    lane = lax.broadcasted_iota(jnp.int32, (ROWS, 128), 1)
    first = jnp.where(row >= end, end, jnp.where(row >= start, start, 0))
    past = jnp.where(row >= end, ROWS, jnp.where(row >= start, end, start))
    bias[...] = jnp.where((lane >= first) & (lane <= row) & (lane < past), 0.0, -1e30)
    half = jnp.where(lane < 64, lane, lane - 64).astype(F32)
    freqs = jnp.exp(half * (-2.0 / HEAD_SIZE * math.log(rope_base)))
    angles = (row - first).astype(F32) * freqs
    cosine[...] = jnp.cos(angles)
    sine[...] = jnp.where(lane < 64, -1.0, 1.0) * jnp.sin(angles)


def weight_gather_kernel(*refs):
    (bounds, w_q, w_k, w_v, w_o, dense, norm_a, norm_m, q_gain, k_gain) = refs[:10]
    (attn_0, attn_1, dense_all, gains_all, cosine, sine, bias) = refs[10:17]
    shard, gains, send, recv, sems = refs[17:]
    place = Place()
    sib = place.sibling()
    p, z, x = place.pipe, place.at["z"], place.at["x"]
    wait_loads()
    shard[:, pl.ds(0, 1024)] = w_q[...]
    shard[:, pl.ds(1024, 128)] = w_k[...]
    shard[:, pl.ds(1152, 128)] = w_v[...]
    shard[:, pl.ds(QKV, 1024)] = w_o[...].T
    gains[...] = jnp.zeros((8, WIDTH), F32)
    gains[pl.ds(0, 1), :] = norm_a[...]
    gains[pl.ds(1, 1), :] = norm_m[...]
    gains[pl.ds(2, 1), pl.ds(0, 128)] = q_gain[...]
    gains[pl.ds(2, 1), pl.ds(128, 128)] = k_gain[...]
    greet(around(place, "xz") + [sib])

    def attn_block(attn, tile):
        def block(wanted, half):
            where = tuple(slice(None) if wanted[a] is None else wanted[a] for a in ("z", "x"))
            return attn.at[where + tile.at(half)]

        return block

    def dense_block(wanted, half):
        where = (p,) + tuple(slice(None) if wanted[a] is None else wanted[a] for a in ("z", "x"))
        rs = slice(None) if half is None else pl.ds(half * 2, 2)
        return dense_all.at[where + (rs,)]

    def run(net, order, block, first, seen):
        wanted = {axis: place.at[axis] for axis in order}
        for number, axis in enumerate(order):
            held = dict(wanted)

            def part(i, half, held=held, axis=axis):
                return block({**held, axis: i}, half)

            yield from gather_ring(
                net,
                place,
                axis,
                part,
                first if number == 0 else None,
                None if seen is None else functools.partial(seen, number, part),
            )
            wanted[axis] = None

    def dense_run(net):
        passed = [net.copy(dense, dense_all.at[p, z, x], sib), net.copy(gains, gains_all.at[p], sib)]

        def seen(number, part, i):
            passed.append(net.copy(part(i, None), part(i, None), sib))

        yield from run(net, ("x", "z"), dense_block, dense, seen)
        for made in passed:
            made.wait_recv()

    placed = [
        pltpu.make_async_copy(dense, dense_all.at[p, z, x], sems.at[0]),
        pltpu.make_async_copy(gains, gains_all.at[p], sems.at[1]),
    ]
    for made in placed:
        made.start()
    placed[0].wait()
    def rings(net, attn, seen):
        return [
            run(
                net,
                WORDERS[sub[0]],
                attn_block(attn, WTILES[sub]),
                shard.at[WTILES[sub].at()],
                None if seen is None else functools.partial(seen, i),
            )
            for i, sub in enumerate(WSUBS)
        ]

    def own_block(attn, tile):
        return attn.at[(z, x) + tile.at()]

    @pl.when(p == 0)
    def _():
        net_d = Net(send, recv)
        net_w = Net(send, recv, DENSE_COPIES)
        passing = Net(send, recv, DENSE_COPIES + RING_COPIES)
        made = pltpu.make_async_copy(shard, attn_0.at[z, x], sems.at[2])
        made.start()
        counts = [0] * len(WSUBS)

        def pass_on(sub, number, part, i):
            at = sub * 7 + 1 + counts[sub]
            counts[sub] += 1
            crossing = passing.describe(part(i, None), part(i, None), sib, at)
            crossing.start()
            passing.made.append(crossing)

        steps = rings(net_w, attn_0, pass_on)
        for step in steps:
            next(step)
        write_tables(bounds, p, cosine, sine, bias)
        for i, sub in enumerate(WSUBS):
            crossing = passing.describe(
                shard.at[WTILES[sub].at()], own_block(attn_0, WTILES[sub]), sib, i * 7
            )
            crossing.start()
            passing.made.append(crossing)
        made.wait()
        together(steps + [dense_run(net_d)])
        for net in (net_d, net_w, passing):
            net.finish()

    @pl.when(p == 1)
    def _():
        net_d = Net(send, recv)
        net_w = Net(send, recv, DENSE_COPIES)
        passing = Net(send, recv, DENSE_COPIES + RING_COPIES)
        made = pltpu.make_async_copy(shard, attn_1.at[z, x], sems.at[2])
        made.start()
        write_tables(bounds, p, cosine, sine, bias)
        together([dense_run(net_d)])

        def receive(number):
            for i, sub in enumerate(WSUBS):
                order = WORDERS[sub[0]]
                wanted = {axis: place.at[axis] for axis in order}
                if number == 0:
                    spot = own_block(attn_0, WTILES[sub])
                    passing.describe(spot, spot, sib, i * 7).wait_recv()
                else:
                    wanted[order[0]] = None
                for k, by in enumerate((-1, 1, 2)):
                    axis = order[number]
                    spot = attn_block(attn_0, WTILES[sub])(
                        {**wanted, axis: place.step(axis, by)}, None
                    )
                    passing.describe(spot, spot, sib, i * 7 + 1 + 3 * number + k).wait_recv()

        receive(0)
        made.wait()
        steps = rings(net_w, attn_1, None)
        for step in steps:
            next(step)
        receive(1)
        together(steps)
        for net in (net_d, net_w):
            net.finish()

    placed[1].wait()


def weight_gather(*args):
    attn = jax.ShapeDtypeStruct((RING, RING, ROWS, ATT), BF)
    table = jax.ShapeDtypeStruct((ROWS, 128), F32)
    return call(
        with_sem(weight_gather_kernel),
        7,
        [
            attn,
            attn,
            jax.ShapeDtypeStruct((2, RING, RING, RING, OWN, 128), F32),
            jax.ShapeDtypeStruct((2, 8, WIDTH), F32),
            table,
            table,
            table,
        ],
        [pltpu.SMEM] + [LOAD] * 9,
        [ANY] * 4 + [VM] * 3,
        [
            VM((ROWS, ATT), BF),
            VM((8, WIDTH), F32),
            pltpu.SemaphoreType.DMA((3,)),
        ],
        args,
        DENSE_COPIES + RING_COPIES + PASS_COPIES,
    )


def sum_everywhere(net, place, value, slots, pair, total):
    current = value[...]
    for number, axis in enumerate("yxz"):
        slot = slots.at[number]
        slot[place.at[axis]] = current

        def block(i, half, slot=slot):
            return slot.at[i] if half is None else slot.at[i, pl.ds(half, 1)]

        yield from gather_ring(net, place, axis, block)
        current = (slot[0] + slot[1]) + (slot[2] + slot[3])
    pair[place.pipe] = current
    crossed = net.copy(pair.at[place.pipe], pair.at[place.pipe], place.sibling())
    yield
    crossed.wait_recv()
    total[...] = pair[0] + pair[1]


TAIL_COPIES = 12 + 8 + 13 + 48
TRADES = 9
TAIL_SUBS = [
    (order[::-1], Tile(0, ROWS, lo, width, True))
    for order, lo, width in (
        (WORDERS[0], 1280, 512),
        (WORDERS[1], 1792, 512),
        (WORDERS[0], 0, 640),
        (WORDERS[1], 640, 640),
    )
]


def tail_kernel(*refs):
    refs = list(refs)
    base, dmid, gains, d_branch_0, qkv_0 = refs[:5]
    tables, gain_rows, on_core = refs[5:8], refs[8:12], refs[12:14]
    gain = gains.at[0, pl.ds(0, 1)]
    by_layer = [refs[14:19], refs[19:27]]
    given_1, stored = refs[27], refs[28:32]
    out, given_0, total = refs[32:35]
    came = refs[35:39]
    came_given, grads_out = refs[39], refs[40:42]
    part, d_qkv_v, d_gains = refs[42:45]
    both, hidden, g_all, x_all, gw_in, gw_down, turned = refs[45:52]
    attn_sems, refs = refs[52], refs[53:]
    by_layer[0].insert(1, d_qkv_v)
    by_layer[0][4:4] = [gw_in, gw_down]
    near, refs = state_bufs(refs[:8]), refs[8:]
    held, ops, part_w = refs[0], refs[1:5], refs[5]
    *bufs, slots, pair, value_v, tally, sems, send, recv = refs[6:]
    bufs = [[[bufs.pop(0) for _ in range(4)] for _ in range(2)] for sub in TAIL_SUBS]
    place = Place()
    sib = place.sibling()
    net = Net(send, recv)
    trade = Net(send, recv, TAIL_COPIES)
    mine, theirs = pl.ds(0, ROWS), pl.ds(ROWS, ROWS)
    targets = [op.at[theirs] for op in ops] + list(came)

    def owed(layer, which):
        return [
            trade.describe(by_layer[layer][i], targets[i], sib, i) for i in which
        ]

    w_out, w_qkv = g_all.at[EVERY + (pl.ds(0, 1024),)], x_all.at[EVERY + (pl.ds(0, QKV),)]
    fetched_w = fetch_attention(on_core, [(QKV, w_out), (0, w_qkv)], attn_sems)

    def exchange(which):
        for core in range(2):

            @pl.when(place.pipe == core)
            def _(core=core):
                for i in which:
                    pltpu.make_async_copy(by_layer[core][i], ops[i].at[mine], sems.at[i]).start()
                for made in owed(1 - core, which):
                    made.start()

    greet(around(place, "xyz") + [sib])
    exchange((2, 3))
    attention_backward(
        0,
        d_branch_0,
        qkv_0,
        fetched_w,
        w_out,
        w_qkv,
        gains,
        tables,
        part,
        d_qkv_v,
        d_gains,
    )
    exchange((0, 1))
    loads = [
        pltpu.make_async_copy(src, dst, attn_sems.at[2 + i])
        for i, (src, dst) in enumerate(zip(stored, (both, hidden, g_all, x_all)))
    ]
    for made in loads:
        made.start()
    value_v[...] = jnp.zeros((2, GAIN_ROWS, 128), F32)
    for layer, row, source in ((0, 16, 0), (1, 0, 1), (1, 16, 2)):
        for i in range(16):
            value_v[layer, pl.ds(row + i, 1), :] = gain_rows[source][:, pl.ds(i * 128, 128)]
    value_v[0, pl.ds(32, 8), :] = d_gains[...]
    value_v[1, pl.ds(32, 8), :] = gain_rows[3][...]
    tally[...] = jnp.zeros((1, WIDTH), F32)

    def state_run():
        def put(t, rs, rows):
            held[t, rs, :] = rows

        yield from in_turn([reduce_tensor(net, place, stream, part, near) for stream in range(2)])
        for stream in range(2):
            state_back(place, stream, base, dmid, gain, near, tally, put)
        for i in range(16):
            value_v[0, pl.ds(i, 1), :] = tally[:, pl.ds(i * 128, 128)]
        yield from in_turn([gather_tensor(net, place, stream, held) for stream in range(2)])

        @pl.when(place.pipe == 1)
        def _():
            trade.describe(held, came_given, sib, 8).start()

        yield from sum_everywhere(net, place, value_v, slots, pair, total)

    state_step = state_run()
    next(state_step)
    steps = []

    def start_reduce(which):
        for sub in which:
            order, tile = TAIL_SUBS[sub]

            def source(wanted, half, tile=tile):
                where = tuple(wanted.get(a, slice(None)) for a in ("z", "x"))
                return part_w.at[where + tile.at(half)]

            step = reduce_all(net, place, order, ("z", "x"), source, tile, bufs[sub])
            next(step)
            steps.append(step)

    for left, right, lo, width, subs in ((3, 2, QKV, 1024, (0, 1)), (0, 1, 0, QKV, (2, 3))):
        for i in (left, right):
            pltpu.make_async_copy(by_layer[0][i], ops[i].at[mine], sems.at[i]).wait()
            trade.describe(ops[i].at[theirs], targets[i], sib, i).wait_recv()

        def product(i, _, left=left, right=right, lo=lo, width=width):
            dims = pl.ds(pl.multiple_of(i * 512, 512), 512)
            made = dot_tn(ops[left][:, dims], ops[right][...]).astype(BF)
            part_w[i, :, :, pl.ds(lo, width)] = made.reshape(RING, ROWS, width)
            return 0

        lax.fori_loop(0, RING, product, 0)
        start_reduce(subs)
    for core in range(2):

        @pl.when(place.pipe == core)
        def _(core=core):
            for made in owed(1 - core, (6, 7)):
                made.start()
            if core == 0:
                trade.describe(given_1, came_given, sib, 8).start()

    for made in loads:
        made.wait()
    fill = weight_grads(
        ((hidden, 0, g_all, gw_down), (both, 0, x_all, gw_in), (both, HIDDEN, x_all, gw_in)), turned
    )
    for number in range(6):
        next(fill)
        if number % 2:
            next(state_step)
    for step in steps:
        next(step)
    for number in range(6):
        next(fill)
        if number % 2:
            next(state_step)
    stores = [
        pltpu.make_async_copy(src, dst, attn_sems.at[i])
        for i, (src, dst) in enumerate(zip((gw_in, gw_down), grads_out))
    ]
    for made in stores:
        made.start()
    for core in range(2):

        @pl.when(place.pipe == core)
        def _(core=core):
            for made in owed(1 - core, (4, 5)):
                made.start()

    together([state_step] + steps)
    for (_, tile), buf in zip(TAIL_SUBS, bufs):
        out[tile.at()] = buf[-1][2][...].astype(F32)
    given_0[...] = held[...]
    net.finish()
    for core in range(2):

        @pl.when(place.pipe == core)
        def _(core=core):
            for made in owed(1 - core, range(8)):
                made.wait_send()
            source = given_1 if core == 0 else held
            trade.describe(source, came_given, sib, 8).wait_send()

    for made in stores:
        made.wait()
    for i in range(4, 8):
        trade.describe(targets[i], targets[i], sib, i).wait_recv()
    trade.describe(came_given, came_given, sib, 8).wait_recv()


def tail(base, dmid, gains, d_branch, qkv, tables, gain_rows, on_core, by_layer, given_1, stored):
    shapes = [x.shape for x in by_layer[1]]
    return call(
        tail_kernel,
        8,
        [
            jax.ShapeDtypeStruct((ROWS, ATT), F32),
            jax.ShapeDtypeStruct((RING, OWN, WIDTH), BF),
            jax.ShapeDtypeStruct((2, GAIN_ROWS, 128), F32),
        ]
        + [jax.ShapeDtypeStruct(shape, BF) for shape in shapes[4:]]
        + [jax.ShapeDtypeStruct((RING, OWN, WIDTH), BF)]
        + [jax.ShapeDtypeStruct((768, WIDTH), BF), jax.ShapeDtypeStruct((HIDDEN, WIDTH), BF)],
        [Load((RING, OWN, WIDTH), of_pipe)] + [LOAD] * 11 + [ANY] * 20,
        [VM] * 3 + [ANY] * 7,
        [
            VM((RING, OWN, WIDTH), BF),
            VM((ROWS, QKV), BF),
            VM((8, 128), F32),
            VM((RING, RING, RING, OWN, 768), BF),
            VM((RING, RING, RING, OWN, HIDDEN), BF),
            VM(TOKENS_ALL, BF),
            VM(TOKENS_ALL, BF),
            VM((768, WIDTH), BF),
            VM((HIDDEN, WIDTH), BF),
            VM((HIDDEN, 2048), BF),
            pltpu.SemaphoreType.DMA((6,)),
        ]
        + state_scratch()
        + [VM((RING, OWN, WIDTH), BF)]
        + [VM((2 * ROWS, shape[1]), BF) for shape in shapes[:4]]
        + [VM((RING, RING, ROWS, ATT), BF)]
        + flat([reduce_scratch(2, tile) for _, tile in TAIL_SUBS])
        + [
            VM((3, RING, 2, GAIN_ROWS, 128), F32),
            VM((2, 2, GAIN_ROWS, 128), F32),
            VM((2, GAIN_ROWS, 128), F32),
            VM((1, WIDTH), F32),
            pltpu.SemaphoreType.DMA((4,)),
        ],
        (
            base.reshape(2, RING, OWN, WIDTH),
            dmid,
            gains,
            d_branch,
            qkv,
            *tables,
            *gain_rows,
            *on_core,
            *by_layer[0],
            *by_layer[1],
            given_1,
            *stored,
        ),
        TAIL_COPIES + TRADES,
    )


def write_kernel(*refs):
    refs = list(refs)
    attn, total = refs[:2]
    in_0, in_1, in_came, down_0, down_1, down_came = refs[2:8]
    act_0, act_1, act_came, given_0, given_1, given_came = refs[8:14]
    d_gate, d_up, d_down, acts, givens, d_query, d_key, d_value, d_out = refs[14:23]
    d_norm_a, d_norm_m, d_q, d_k = refs[23:27]
    pieces, pieces_came, sums, rows, rows_f, sem_in, sem_out = refs[27:]
    pipe = lax.axis_index("pipe")
    adds = []

    def load(i):
        which, lo = divmod(i * 192, HIDDEN)
        own = (in_0, in_1) if which < 2 else (down_0, down_1)
        came = in_came if which < 2 else down_came
        rs = pl.ds(lo + (HIDDEN if which == 1 else 0), 192)
        for core in range(2):

            @pl.when(pipe == core)
            def _(source=own[core]):
                pltpu.make_async_copy(source.at[rs], pieces.at[i], sem_in.at[2 * i]).start()

        pltpu.make_async_copy(came.at[rs], pieces_came.at[i], sem_in.at[2 * i + 1]).start()
        adds.append((d_gate, d_up, d_down)[which].at[pl.ds(lo, 192)])

    sources = ((act_0, act_1), (given_0, given_1))

    def load_rows(k):
        for core in range(2):

            @pl.when(pipe == core)
            def _(source=sources[k][core]):
                pltpu.make_async_copy(source, rows.at[2 * k], sem_in.at[12 + 2 * k]).start()

        came = (act_came, given_came)[k]
        pltpu.make_async_copy(came, rows.at[2 * k + 1], sem_in.at[13 + 2 * k]).start()

    for i in range(3):
        load(i)
    stores = []
    wait_loads()
    for i in range(16):
        d_norm_a[:, pl.ds(i * 128, 128)] = total[pipe, pl.ds(i, 1), :]
        d_norm_m[:, pl.ds(i * 128, 128)] = total[pipe, pl.ds(16 + i, 1), :]
    d_q[...] = total[pipe, pl.ds(32, 1), :]
    d_k[...] = total[pipe, pl.ds(33, 1), :]
    d_query[...] = attn[:, pl.ds(0, 1024)]
    d_key[...] = attn[:, pl.ds(1024, 128)]
    d_value[...] = attn[:, pl.ds(1152, 128)]
    d_out[...] = attn[:, pl.ds(QKV, 1024)].T
    for i in range(6):
        pltpu.make_async_copy(in_0.at[pl.ds(0, 192)], pieces.at[i], sem_in.at[2 * i]).wait()
        pltpu.make_async_copy(in_0.at[pl.ds(0, 192)], pieces_came.at[i], sem_in.at[2 * i + 1]).wait()
        if i < 3:
            load(i + 3)
        elif i < 5:
            load_rows(i - 3)

        def each(j, _, i=i):
            rs = pl.ds(pl.multiple_of(j * 32, 32), 32)
            sums[i, rs, :] = pieces[i, rs, :].astype(F32) + pieces_came[i, rs, :].astype(F32)
            return 0

        lax.fori_loop(0, 6, each, 0)
        made = pltpu.make_async_copy(sums.at[i], adds[i], sem_out.at[i])
        made.start()
        stores.append(made)
    for k, out in enumerate((acts, givens)):
        for n in range(2):
            i = 2 * k + n
            pltpu.make_async_copy(act_0, rows.at[i], sem_in.at[12 + i]).wait()

            def each(j, _, i=i):
                rs = pl.ds(pl.multiple_of(j * 16, 16), 16)
                rows_f[i, rs, :] = rows[i, rs, :].astype(F32)
                return 0

            lax.fori_loop(0, 8, each, 0)
            spot = out.at[pipe if n == 0 else 1 - pipe]
            made = pltpu.make_async_copy(rows_f.at[i], spot, sem_out.at[6 + i])
            made.start()
            stores.append(made)
    for made in stores:
        made.wait()


def write_outputs(*args):
    kernel, held, kinds = loading(write_kernel, [LOAD] * 2 + [ANY] * 12, args)
    return pl.pallas_call(
        kernel,
        out_shape=[jax.ShapeDtypeStruct((HIDDEN, WIDTH), F32)] * 3
        + [jax.ShapeDtypeStruct((2, ROWS, WIDTH), F32)] * 2
        + [
            jax.ShapeDtypeStruct((ROWS, 1024), F32),
            jax.ShapeDtypeStruct((ROWS, 128), F32),
            jax.ShapeDtypeStruct((ROWS, 128), F32),
            jax.ShapeDtypeStruct((1024, ROWS), F32),
            jax.ShapeDtypeStruct((1, WIDTH), F32),
            jax.ShapeDtypeStruct((1, WIDTH), F32),
            jax.ShapeDtypeStruct((1, 128), F32),
            jax.ShapeDtypeStruct((1, 128), F32),
        ],
        in_specs=[pl.BlockSpec(memory_space=kind) for kind in kinds],
        out_specs=[pl.BlockSpec(memory_space=ANY)] * 5 + [pl.BlockSpec(memory_space=VM)] * 8,
        scratch_shapes=[
            VM((6, 192, WIDTH), BF),
            VM((6, 192, WIDTH), BF),
            VM((6, 192, WIDTH), F32),
            VM((4, ROWS, WIDTH), BF),
            VM((4, ROWS, WIDTH), F32),
            pltpu.SemaphoreType.DMA((16,)),
            pltpu.SemaphoreType.DMA((10,)),
        ]
        + held,
        compiler_params=pltpu.CompilerParams(vmem_limit_bytes=60 * 2**20),
        cost_estimate=pl.CostEstimate(flops=0, bytes_accessed=24 * 2**20, transcendentals=0),
    )(*args)


def dot_nn(a, b):
    return lax.dot_general(a, b, (((1,), (0,)), ((), ())), preferred_element_type=F32)


def dot_nt(a, b):
    return lax.dot_general(a, b, (((1,), (1,)), ((), ())), preferred_element_type=F32)


def dot_tn(a, b):
    return lax.dot_general(a, b, (((0,), (0,)), ((), ())), preferred_element_type=F32)


def stack_heads(values, count):
    return jnp.concatenate([values[:, h * 128 : (h + 1) * 128] for h in range(count)], axis=0)


def unstack_heads(values, count):
    return jnp.concatenate([values[h * ROWS : (h + 1) * ROWS, :] for h in range(count)], axis=1)


def turn(values, cosine, sine):
    return values * cosine + pltpu.roll(values, 64, 1) * sine


def over_heads(table):
    return jnp.concatenate([table] * 8, axis=0)


SCORE_SCALE = HEAD_SIZE ** (-0.5)


def fetch_attention(sources, parts, sem):
    made = []
    for number, (lo, spot) in enumerate(parts):
        cs = pl.ds(lo, spot.shape[-1])
        for core, source in enumerate(sources):

            @pl.when(lax.axis_index("pipe") == core)
            def _(source=source):
                source = source.at[EVERY + (cs,)]
                pltpu.make_async_copy(source, spot, sem.at[number]).start()

        made.append(pltpu.make_async_copy(sources[0].at[EVERY + (cs,)], spot, sem.at[number]))
    return made


EVERY = (slice(None),) * 4


def columns(spot):
    return spot[...].reshape(WIDTH, spot.shape[-1])


def head_gains(gains, layer):
    row = pl.ds(2, 1)
    return gains[layer, row, pl.ds(0, 128)], gains[layer, row, pl.ds(128, 128)]


def attention_forward(layer, state, fetched, parts, gains, tables, branch, normed, qkv, attended):
    q_gain, k_gain = head_gains(gains, layer)
    cos, sin, bias = (table[...] for table in tables)
    rows = state[...].reshape(ROWS, WIDTH).astype(F32)
    normed[...] = (rows * inv_rms(rows) * gains[layer, pl.ds(0, 1), :]).astype(BF)
    fetched[0].wait()
    qkv[...] = dot_nn(normed[...], columns(parts[0][1]))
    query = stack_heads(qkv[:, pl.ds(0, 1024)], 8)
    key = qkv[:, pl.ds(1024, 128)]
    value = qkv[:, pl.ds(1152, 128)].astype(BF)
    q_rot = turn(query * inv_rms(query) * q_gain, over_heads(cos), over_heads(sin)).astype(BF)
    k_rot = turn(key * inv_rms(key) * k_gain, cos, sin).astype(BF)
    scores = dot_nt(q_rot, k_rot) * SCORE_SCALE + over_heads(bias)
    grown = jnp.exp(scores - jnp.max(scores, axis=-1, keepdims=True))
    probs = (grown / jnp.sum(grown, axis=-1, keepdims=True)).astype(BF)
    attended[...] = unstack_heads(dot_nn(probs, value), 8).astype(BF)
    total = None
    for made, (lo, spot) in zip(fetched[1:], parts[1:]):
        made.wait()
        heads = attended[:, pl.ds(lo - QKV, spot.shape[-1])]
        term = dot_nt(heads, columns(spot))
        total = term if total is None else total + term
    branch[...] = total.astype(BF).reshape(RING, OWN, WIDTH)


def attention_backward(layer, d_branch, qkv, fetched, w_out, w_qkv, gains, tables, d_normed, d_qkv, d_gains):
    q_gain, k_gain = head_gains(gains, layer)
    cos, sin, bias = (table[...] for table in tables)
    cos8, sin8 = over_heads(cos), over_heads(sin)
    query = stack_heads(qkv[:, pl.ds(0, 1024)], 8)
    key = qkv[:, pl.ds(1024, 128)]
    value = qkv[:, pl.ds(1152, 128)].astype(BF)
    q_rot = turn(query * inv_rms(query) * q_gain, cos8, sin8).astype(BF)
    k_rot = turn(key * inv_rms(key) * k_gain, cos, sin).astype(BF)
    scores = dot_nt(q_rot, k_rot) * SCORE_SCALE + over_heads(bias)
    grown = jnp.exp(scores - jnp.max(scores, axis=-1, keepdims=True))
    prob = grown / jnp.sum(grown, axis=-1, keepdims=True)
    fetched[0].wait()
    d_att = dot_nn(d_branch[...].reshape(ROWS, WIDTH), columns(w_out)).astype(BF)
    d_att = stack_heads(d_att, 8)
    d_prob = dot_nt(d_att, value)
    d_value = dot_tn(prob.astype(BF), d_att)
    delta = jnp.sum(prob * d_prob, axis=-1, keepdims=True)
    d_scores = (prob * (d_prob - delta)).astype(BF)
    d_q_rot = dot_nn(d_scores, k_rot) * SCORE_SCALE
    d_k_rot = dot_tn(d_scores, q_rot) * SCORE_SCALE
    d_query, q_rows = norm_back(turn(d_q_rot, cos8, -sin8), query, q_gain)
    d_key, k_rows = norm_back(turn(d_k_rot, cos, -sin), key, k_gain)
    d_qkv[:, pl.ds(0, 1024)] = unstack_heads(d_query, 8).astype(BF)
    d_qkv[:, pl.ds(1024, 128)] = d_key.astype(BF)
    d_qkv[:, pl.ds(1152, 128)] = d_value.astype(BF)
    fetched[1].wait()
    made = dot_nt(d_qkv[...], columns(w_qkv))
    d_normed[...] = made.astype(BF).reshape(RING, OWN, WIDTH)
    d_gains[...] = jnp.zeros((8, 128), F32)
    d_gains[pl.ds(0, 1), :] = jnp.sum(q_rows, axis=0, keepdims=True)
    d_gains[pl.ds(1, 1), :] = jnp.sum(k_rows, axis=0, keepdims=True)


def plane_at(chunk, i):
    last = ORDERS[chunk][-1]
    return tuple(i if axis == last else slice(None) for axis in ("z", "x", "y"))


def fetch_experts(place, layer, own, other, dst, sems):
    spots = [dst[0].at[pl.ds(0, 2)], dst[0].at[pl.ds(2, 2)], dst[1]]
    for refs, mine in ((own, True), (other, False)):
        here = place.pipe == layer if mine else place.pipe != layer

        @pl.when(here)
        def _(refs=refs):
            for i, (ref, spot) in enumerate(zip(refs, spots)):
                pltpu.make_async_copy(ref, spot, sems.at[i]).start()

    return [
        pltpu.make_async_copy(ref, spot, sems.at[i]) for i, (ref, spot) in enumerate(zip(own, spots))
    ]


F, T = "f", "t"
FORWARD = (0, 1) * 5 + (
    *(0, 0, 0, 1, 0, 0, 0, 0, 0, 0, 1, 1, 0, 1, 1, 0, 1, 1, 1),
    *(0, 1, 0, 1, 0, 1, 0, 0, 1, 0, 1, 0, 1, 1, 1, 1, 1),
)
BACKWARD_0 = (
    *(0, 1, 0, 1, 0, 0, 1, 1, 0, 0, 0, 0, 1, 0, 1, 1, 0, 0, 0, 0),
    *(1, 1, 1, 0, 0, 1, 1, 1, F, F, 0, F, 1, F, T, F, 0, 1, 0, F),
    *(1, T, F, F, 0, F, 1, F, 0, T, F, 1, 0, T, 1, T, 1, 0, T, 1),
    *(T, 0, F, T, 1, T, 1),
)
BACKWARD_1 = (
    *(0, 0, 0, 1, 1, 0, 1, 1, 0, 0, 0, 0, 0, 1, 0, 1, 0, 0, 0, 0),
    *(1, 1, 1, 1, 0, 0, 1, 1, 1, 1, F, T, F, 0, 1, T, F, 0, F, F),
    *(1, 0, F, 0, 1, 0, T, 1, F, F, 1, F, T, 1, F, 0, T, 1, T, F),
    *(T, 1, T, F, 1, 0, T),
)


def pick_weight(place, rows, lane):
    first = EXPERTS * place.pipe + 2 * (place.at["z"] * RING + place.at["x"])
    column = lax.broadcasted_iota(jnp.int32, rows.shape, 2)
    low = jnp.sum(jnp.where(column == first, rows, 0.0), axis=2, keepdims=True)
    high = jnp.sum(jnp.where(column == first + 1, rows, 0.0), axis=2, keepdims=True)
    return jnp.where(lane < 192, low, high)


def stream_steps(net, place, stream, spread_rows, own, gathered, compute, mix, part, bufs, make, finish, held):
    yield from spread_rows(stream)
    gather = gather_tokens(net, place, stream, own, gathered)
    for _ in range(5):
        next(gather)
        yield
    for chunk in range(3):
        compute(chunk, stream, 0)
    yield
    next(gather)
    yield
    for by in (-1, 1):
        for chunk in range(3):
            compute(chunk, stream, by)
        yield
    together([gather])
    yield
    for chunk in range(3):
        compute(chunk, stream, 2)
    yield
    mix(stream)
    yield
    yield from reduce_tokens(net, place, stream, part, bufs, make)
    finish(stream)
    yield from gather_tensor(net, place, stream, held)


def layer_forward_kernel(layer, *refs):
    refs = list(refs)
    (base, gains, dense), tables, on_core, refs = refs[:3], refs[3:6], refs[6:8], refs[4:]
    gain = gains.at[layer, pl.ds(1, 1)]
    own_w, other_w = refs[4:7], refs[7:10]
    refs = refs[10:]
    if layer == 0:
        attn_1, refs = refs[0], refs[1:]
    out, middle, kept, state = refs[:4]
    results, refs = refs[4:7], refs[7:]
    if layer == 0:
        attn_came, refs = refs[0], refs[1:]
    part, *attn_v, rest_w, attn_sems = refs[:6]
    refs = refs[6:]
    near, refs = state_bufs(refs[:8]), refs[8:]
    (own, held, x_all, part_all, acc, kept_v, hidden, w_in, w_down, spread) = refs[:10]
    *bufs, sems, send, recv = refs[10:]
    bufs = token_bufs(bufs)
    place = Place()
    net = Net(send, recv)
    fetched = fetch_experts(place, layer, own_w, other_w, (w_in, w_down), sems)
    fetched.append(pltpu.make_async_copy(dense.at[layer], spread, sems.at[5]))
    fetched[-1].start()
    parts = [
        (0, part_all.at[EVERY + (pl.ds(0, QKV),)]),
        (QKV, part_all.at[EVERY + (pl.ds(QKV, WIDTH - QKV),)]),
        (WIDTH, rest_w),
    ]
    fetched_w = fetch_attention(on_core, parts, attn_sems)

    def attend():
        attention_forward(layer, base, fetched_w, parts, gains, tables, part, *attn_v)

    if layer == 0:
        crossing = net.describe(attn_1, attn_came, place.sibling(), FORWARD_COPIES)
        greet_sibling(place, around(place, "xyz"), attend)

        @pl.when(place.pipe == 1)
        def _():
            crossing.start()

    else:
        greet(around(place, "xyz"), attend)
    attn_saved = [
        pltpu.make_async_copy(src, dst, attn_sems.at[3 + i])
        for i, (src, dst) in enumerate(zip(attn_v, results))
    ]
    for made in attn_saved:
        made.start()
    z, x, t = place.at["z"], place.at["x"], place.at["y"]

    def clear(i, _):
        acc[lax.div(i, 16), lax.rem(lax.div(i, 4), 4), lax.rem(i, 4)] = jnp.zeros((OWN, 768), F32)
        return 0

    def spread_rows(stream):
        yield from reduce_tensor(net, place, stream, part, near)
        rs = pl.ds(stream * 16, 16)
        value = base[t, rs, :].astype(F32) + near[stream][2][...].astype(F32)
        middle[rs, :] = value
        rounded = (value * inv_rms(value) * gain[...]).astype(BF)
        own[rs, :] = rounded
        x_all[z, x, t, rs, :] = rounded

    def gate_up(chunk, stream, by):
        rs, cs = TILES[chunk, stream].at()
        at = plane_at(chunk, place.step(ORDERS[chunk][-1], by)) + (rs,)
        rows = x_all[at + (cs,)].reshape(256, cs.size)
        made = dot_nt(rows, w_in[:, :, cs].reshape(768, cs.size))
        acc[at] = acc[at] + made.reshape(RING, RING, 16, 768)

    lane = lax.broadcasted_iota(jnp.int32, (RING, 16, HIDDEN), 2)
    saved = [
        pltpu.make_async_copy(x_all, out, sems.at[3]),
        pltpu.make_async_copy(kept_v, kept, sems.at[4]),
    ]

    mixed = []

    def mix(stream):
        def tile(i, _):
            at = (lax.div(i, 4), lax.rem(i, 4), slice(None), pl.ds(stream * 16, 16))
            both = acc[at]
            kept_v[at] = both.astype(BF)
            gate, up = both[:, :, :HIDDEN], both[:, :, HIDDEN:]
            weight = pick_weight(place, spread[at], lane)
            hidden[at] = (gate * jax.nn.sigmoid(gate) * up * weight).astype(BF)
            return 0

        lax.fori_loop(0, 16, tile, 0)
        mixed.append(stream)
        if len(mixed) == 2:
            for made in saved:
                made.start()

    def down(chunk, stream, by):
        rs, cs = TILES[chunk, stream].at()
        at = plane_at(chunk, place.step(ORDERS[chunk][-1], by)) + (rs,)
        made = dot_nn(hidden[at].reshape(256, HIDDEN), w_down[:, :, cs].reshape(HIDDEN, cs.size))
        part_all[at + (cs,)] = made.astype(BF).reshape(RING, RING, 16, cs.size)

    def finish(stream):
        rs = pl.ds(stream * 16, 16)
        held[t, rs, :] = (middle[rs, :] + token_sums(bufs, stream)).astype(BF)

    steps = {
        i: stream_steps(
            net, place, i, spread_rows, own, x_all, gate_up, mix, part_all, bufs, down, finish, held
        )
        for i in range(2)
    }
    for i in range(2):
        next(steps[i])
    lax.fori_loop(0, 64, clear, 0)
    for made in fetched:
        made.wait()
    run_schedule(FORWARD, steps)
    net.finish()
    state[...] = held[...]
    for made in saved + attn_saved:
        made.wait()
    if layer == 0:

        @pl.when(place.pipe == 0)
        def _():
            crossing.wait_recv()

        @pl.when(place.pipe == 1)
        def _():
            crossing.wait_send()


FORWARD_COPIES = 12 + GATHER_COPIES + REDUCE_COPIES + 8


def layer_forward(layer, base, gains, dense, tables, on_core, own_w, other_w, *attn_1):
    outs = [
        jax.ShapeDtypeStruct(TOKENS_ALL, BF),
        jax.ShapeDtypeStruct((OWN, WIDTH), F32),
        jax.ShapeDtypeStruct((RING, RING, RING, OWN, 768), BF),
        jax.ShapeDtypeStruct((RING, OWN, WIDTH), BF),
        jax.ShapeDtypeStruct((ROWS, WIDTH), BF),
        jax.ShapeDtypeStruct((ROWS, QKV), F32),
        jax.ShapeDtypeStruct((ROWS, 1024), BF),
    ]
    kinds = [ANY, VM, ANY, VM, ANY, ANY, ANY]
    if layer == 0:
        outs.append(jax.ShapeDtypeStruct((RING, RING, ROWS, ATT), BF))
        kinds.append(ANY)
    return call(
        functools.partial(layer_forward_kernel, layer),
        1 + 20 * layer,
        outs,
        [Load((RING, OWN, WIDTH), of_pipe if layer == 0 else None), LOAD, ANY, LOAD, LOAD, LOAD]
        + [ANY] * (8 + len(attn_1)),
        kinds,
        [
            VM((RING, OWN, WIDTH), BF),
            VM((ROWS, WIDTH), BF),
            VM((ROWS, QKV), F32),
            VM((ROWS, 1024), BF),
            VM((RING, RING, RING, OWN, ATT - WIDTH), BF),
            pltpu.SemaphoreType.DMA((6,)),
        ]
        + state_scratch()
        + [
            VM((OWN, WIDTH), BF),
            VM((RING, OWN, WIDTH), BF),
            VM(TOKENS_ALL, BF),
            VM(TOKENS_ALL, BF),
            VM((RING, RING, RING, OWN, 768), F32),
            VM((RING, RING, RING, OWN, 768), BF),
            VM((RING, RING, RING, OWN, HIDDEN), BF),
            VM((4, 192, WIDTH), BF),
            VM((2, 192, WIDTH), BF),
            VM((RING, RING, RING, OWN, 128), F32),
        ]
        + token_scratch()
        + [pltpu.SemaphoreType.DMA((6,))],
        (
            base.reshape(*base.shape[:-2], RING, OWN, WIDTH),
            gains,
            dense,
            *tables,
            *on_core,
            *own_w,
            *other_w,
            *attn_1,
        ),
        FORWARD_COPIES + 1,
        60,
    )


def weight_grads(groups, turned):
    for left, lo, right, out in groups:
        turned[...] = left[EVERY + (pl.ds(lo, HIDDEN),)].reshape(2048, HIDDEN).T
        for j in range(4):
            cs = pl.ds(j * 512, 512)
            made = dot_nn(turned[...], right[EVERY + (cs,)].reshape(2048, 512))
            out[pl.ds(lo, HIDDEN), cs] = made.astype(BF)
            yield


def layer_backward_kernel(layer, *refs):
    refs = list(refs)
    if layer == 1:
        given, refs = refs[0], refs[1:]
    else:
        (base, dmid_next, d_branch_next, qkv_next), refs = refs[:4], refs[4:]
        tables, on_core, refs = refs[:3], refs[3:5], refs[5:]
    (middle, gains, dense, kept, tokens) = refs[:5]
    gain, gain_next = gains.at[layer, pl.ds(1, 1)], gains.at[1, pl.ds(0, 1)]
    own_w, other_w = refs[5:8], refs[8:11]
    dmid, d_branch, tally, d_gain = refs[11:15]
    refs = refs[15:]
    if layer == 1:
        (grad_in, grad_down), refs = refs[:2], refs[2:]
    else:
        operands_out, refs = refs[:3], refs[3:]
    if layer == 0:
        (given_out, d_gain_next, d_qkv_out, d_gains_next), refs = refs[:4], refs[4:]
        (part, d_qkv_v, attn_sems), refs = refs[:3], refs[3:]
        near, refs = state_bufs(refs[:8]), refs[8:]
    (own, held, held_d, g_all, x_all, part_all, part_d, acc, both, hidden, w_in, w_down) = refs[:12]
    spread, refs = refs[12], refs[13:]
    if layer == 1:
        (gw_in, gw_down, turned), refs = refs[:3], refs[3:]
    *bufs, sems, send, recv = refs
    tally_bufs = [[bufs.pop(0) for _ in range(4)] for _ in range(3)]
    bufs = token_bufs(bufs)
    place = Place()
    net = Net(send, recv)
    z, x, t = place.at["z"], place.at["x"], place.at["y"]
    fetched = fetch_experts(place, layer, own_w, other_w, (w_in, w_down), sems)
    d_gain[...] = jnp.zeros((1, WIDTH), F32)
    if layer == 0:
        d_gain_next[...] = jnp.zeros((1, WIDTH), F32)
    mixed = []
    for src, dst, i in ((kept, both, 3), (dense.at[layer], spread, 7)):
        made = pltpu.make_async_copy(src, dst, sems.at[i])
        made.start()
        fetched.append(made)
    attend = None
    if layer == 0:
        w_out = part_all.at[EVERY + (pl.ds(0, 1024),)]
        w_qkv = x_all.at[EVERY + (pl.ds(0, QKV),)]
        fetched_w = fetch_attention(on_core, [(QKV, w_out), (0, w_qkv)], attn_sems)

        def attend():
            attention_backward(
                1,
                d_branch_next,
                qkv_next,
                fetched_w,
                w_out,
                w_qkv,
                gains,
                tables,
                part,
                d_qkv_v,
                d_gains_next,
            )

    greet(around(place, "xyz"), attend)
    if layer == 1:
        token_copy = pltpu.make_async_copy(tokens, x_all, sems.at[4])
        token_copy.start()
    else:
        saving = pltpu.make_async_copy(d_qkv_v, d_qkv_out, attn_sems.at[2])
        saving.start()
        stores = [
            pltpu.make_async_copy(src, dst, sems.at[4 + i])
            for i, (src, dst) in enumerate(zip((both, hidden, g_all), operands_out))
        ]

    def clear(i, _):
        acc[lax.div(i, 16), lax.rem(lax.div(i, 4), 4), lax.rem(i, 4)] = jnp.zeros((OWN, HIDDEN), F32)
        return 0

    def spread_rows(stream):
        rs = pl.ds(stream * 16, 16)
        if layer == 0:

            def put(t, rs, value):
                own[rs, :] = value

            yield from reduce_tensor(net, place, stream, part, near)
            state_back(place, stream, base, dmid_next, gain_next, near, d_gain_next, put)
        else:
            own[rs, :] = given[t, rs, :]
            yield
            yield
        g_all[z, x, t, rs, :] = own[rs, :]

    def back_hidden(chunk, stream, by):
        rs, cs = TILES[chunk, stream].at()
        at = plane_at(chunk, place.step(ORDERS[chunk][-1], by)) + (rs,)
        rows = g_all[at + (cs,)].reshape(256, cs.size)
        made = dot_nt(rows, w_down[:, :, cs].reshape(HIDDEN, cs.size))
        acc[at] = acc[at] + made.reshape(RING, RING, 16, HIDDEN)

    lane = lax.broadcasted_iota(jnp.int32, (RING, 16, HIDDEN), 2)
    column = lax.broadcasted_iota(jnp.int32, (RING, 16, 128), 2)
    expert = 2 * (z * RING + x)

    def mix(stream):
        def tile(i, _):
            at = (lax.div(i, 4), lax.rem(i, 4), slice(None), pl.ds(stream * 16, 16))
            gate = both[at + (pl.ds(0, HIDDEN),)].astype(F32)
            up = both[at + (pl.ds(HIDDEN, HIDDEN),)].astype(F32)
            d_hidden = acc[at]
            sig = jax.nn.sigmoid(gate)
            silu = gate * sig
            value = silu * up
            dots = value * d_hidden
            low = jnp.sum(jnp.where(lane < 192, dots, 0.0), axis=2, keepdims=True)
            high = jnp.sum(jnp.where(lane < 192, 0.0, dots), axis=2, keepdims=True)
            part_d[at] = (
                jnp.where(column == expert, low, 0.0) + jnp.where(column == expert + 1, high, 0.0)
            ).astype(BF)
            weight = pick_weight(place, spread[at], lane)
            d_hidden = d_hidden * weight
            hidden[at] = (value * weight).astype(BF)
            d_gate = d_hidden * up * sig * (1.0 + gate * (1.0 - sig))
            both[at + (pl.ds(0, HIDDEN),)] = d_gate.astype(BF)
            both[at + (pl.ds(HIDDEN, HIDDEN),)] = (d_hidden * silu).astype(BF)
            return 0

        lax.fori_loop(0, 16, tile, 0)
        mixed.append(stream)
        if layer == 0 and len(mixed) == 2:
            given_out[...] = g_all[z, x]
            for made in stores:
                made.start()

    def back_rows(chunk, stream, by):
        rs, cs = TILES[chunk, stream].at()
        at = plane_at(chunk, place.step(ORDERS[chunk][-1], by)) + (rs,)
        made = dot_nn(both[at].reshape(256, 768), w_in[:, :, cs].reshape(768, cs.size))
        part_all[at + (cs,)] = made.astype(BF).reshape(RING, RING, 16, cs.size)

    def tallying():
        yield from reduce_all(
            net,
            place,
            ("x", "z", "y"),
            ("z", "x", "y"),
            token_block(part_d, TALLY_TILE),
            TALLY_TILE,
            tally_bufs,
        )
        held_d[t, :, :] = tally_bufs[-1][2][...]
        yield from gather_ring(net, place, "y", tensor_blocks(held_d, TALLY_TILE))

    def finish(stream):
        rs = pl.ds(stream * 16, 16)
        back, rows = norm_back(token_sums(bufs, stream), middle[rs, :], gain[...])
        value = own[rs, :].astype(F32) + back
        dmid[rs, :] = value
        held[t, rs, :] = value.astype(BF)
        add_rows(d_gain, rows)

    steps = {
        i: stream_steps(
            net,
            place,
            i,
            spread_rows,
            own,
            g_all,
            back_hidden,
            mix,
            part_all,
            bufs,
            back_rows,
            finish,
            held,
        )
        for i in range(2)
    }
    for i in range(2):
        next(steps[i])
    lax.fori_loop(0, 64, clear, 0)
    for made in fetched:
        made.wait()
    steps[T] = tallying()
    if layer == 1:

        def fill():
            token_copy.wait()
            yield from weight_grads(
                (
                    (hidden, 0, g_all, gw_down),
                    (both, 0, x_all, gw_in),
                    (both, HIDDEN, x_all, gw_in),
                ),
                turned,
            )

        steps[F] = fill()
        run_schedule(BACKWARD_1, steps)
        stores = []
        for src, dst, i in ((gw_in, grad_in, 5), (gw_down, grad_down, 6)):
            made = pltpu.make_async_copy(src, dst, sems.at[i])
            made.start()
            stores.append(made)
    else:
        run_schedule([step for step in BACKWARD_0 if step != F], steps)
    net.finish()
    d_branch[...] = held[...]
    tally[...] = held_d[...]
    for made in stores:
        made.wait()
    if layer == 0:
        saving.wait()


def layer_backward(layer, lead, middle, gains, dense, kept, tokens, own_w, other_w):
    outs = [
        jax.ShapeDtypeStruct((OWN, WIDTH), F32),
        jax.ShapeDtypeStruct((RING, OWN, WIDTH), BF),
        jax.ShapeDtypeStruct((RING, OWN, 128), BF),
        jax.ShapeDtypeStruct((1, WIDTH), F32),
    ]
    kinds = [VM, VM, VM, VM]
    if layer == 1:
        outs += [
            jax.ShapeDtypeStruct((768, WIDTH), BF),
            jax.ShapeDtypeStruct((HIDDEN, WIDTH), BF),
        ]
        kinds += [ANY, ANY]
    else:
        outs += [
            jax.ShapeDtypeStruct((RING, RING, RING, OWN, 768), BF),
            jax.ShapeDtypeStruct((RING, RING, RING, OWN, HIDDEN), BF),
            jax.ShapeDtypeStruct(TOKENS_ALL, BF),
        ]
        kinds += [ANY, ANY, ANY]
    scratch = []
    lead_kinds = [Load((RING, OWN, WIDTH), of_pipe)]
    if layer == 0:
        lead_kinds = [LOAD] * 7 + [ANY] * 2
    if layer == 0:
        outs += [
            jax.ShapeDtypeStruct((RING, OWN, WIDTH), BF),
            jax.ShapeDtypeStruct((1, WIDTH), F32),
            jax.ShapeDtypeStruct((ROWS, QKV), BF),
            jax.ShapeDtypeStruct((8, 128), F32),
        ]
        kinds += [VM, VM, ANY, VM]
        scratch = [
            VM((RING, OWN, WIDTH), BF),
            VM((ROWS, QKV), BF),
            pltpu.SemaphoreType.DMA((3,)),
        ]
        scratch += state_scratch()
    scratch = scratch + [
        VM((OWN, WIDTH), BF),
        VM((RING, OWN, WIDTH), BF),
        VM((RING, OWN, 128), BF),
        VM(TOKENS_ALL, BF),
        VM(TOKENS_ALL, BF),
        VM(TOKENS_ALL, BF),
        VM((RING, RING, RING, OWN, 128), BF),
        VM((RING, RING, RING, OWN, HIDDEN), F32),
        VM((RING, RING, RING, OWN, 768), BF),
        VM((RING, RING, RING, OWN, HIDDEN), BF),
        VM((4, 192, WIDTH), BF),
        VM((2, 192, WIDTH), BF),
        VM((RING, RING, RING, OWN, 128), F32),
    ]
    if layer == 1:
        scratch += [VM((768, WIDTH), BF), VM((HIDDEN, WIDTH), BF), VM((HIDDEN, 2048), BF)]
    scratch += flat(reduce_scratch(3, TALLY_TILE)) + token_scratch()
    scratch += [pltpu.SemaphoreType.DMA((8,))]
    return call(
        functools.partial(layer_backward_kernel, layer),
        2 + 20 * layer,
        outs,
        lead_kinds + [LOAD] * 2 + [ANY] * 9,
        kinds,
        scratch,
        (
            *lead,
            middle,
            gains,
            dense,
            kept,
            tokens,
            *own_w,
            *other_w,
        ),
        12 + GATHER_COPIES + REDUCE_COPIES + 18 + 8 + 4,
        62,
    )


def body(
    inputs,
    cotangent,
    doc_bounds,
    routes,
    gates,
    norm_attn,
    norm_moe,
    q_gain,
    k_gain,
    w_query,
    key_matrix,
    value_matrix,
    w_out,
    w_gate,
    w_up,
    w_down,
):
    pipe = lax.axis_index("pipe")
    expert = lax.axis_index("expert")
    tensor = lax.axis_index("tensor")
    own_w = (w_gate[0], w_up[0], w_down[0])
    other_w = tuple(lax.ppermute(w, "pipe", [(0, 1), (1, 0)]) for w in own_w)

    named = routes[0][:, :, :, None] == jnp.arange(EXPERTS, dtype=jnp.int32)
    dense = jnp.sum(jnp.where(named, gates[0][:, :, :, None], 0.0), axis=2)
    dense = jnp.concatenate([dense[0], dense[1], jnp.zeros((ROWS, 64), F32)], axis=1)
    dense = dense.reshape(RING, OWN, 128)
    attn_0, attn_1, dense_all, gains, *layout = weight_gather(
        doc_bounds,
        w_query[0],
        key_matrix[0],
        value_matrix[0],
        w_out[0],
        dense,
        norm_attn,
        norm_moe,
        q_gain,
        k_gain,
    )
    first = pipe == 0

    kept, states = [], [inputs]
    by_rows = (RING, RING, RING, OWN, ATT)
    rows_0, rows_1 = attn_0.reshape(by_rows), attn_1.reshape(by_rows)
    weights_of = [(rows_0, rows_0), None]
    for layer in range(2):
        tokens, middle, both, state, normed, qkv, attended, *came = layer_forward(
            layer,
            states[layer],
            gains,
            dense_all,
            layout,
            weights_of[layer],
            own_w,
            other_w,
            *[attn_1][layer:],
        )
        if layer == 0:
            weights_of[1] = (came[0].reshape(by_rows), rows_1)
        kept.append((normed, qkv, attended, middle, tokens, both))
        states.append(state.reshape(ROWS, WIDTH))

    results, gain_sums = [None, None], [None, None]
    d_branch, d_qkv = [None, None], [None, None]
    for layer in (1, 0):
        normed, qkv, attended, middle, tokens, both = kept[layer]
        if layer == 1:
            lead = (cotangent.reshape(2, RING, OWN, WIDTH),)
        else:
            lead = (
                states[1].reshape(RING, OWN, WIDTH),
                dmid,
                d_branch[1],
                kept[1][1],
                *layout,
                *weights_of[1],
            )
        dmid, d_branch[layer], tally, d_norm_m, *more = layer_backward(
            layer, lead, middle, gains, dense_all, both, tokens, own_w, other_w
        )
        results[layer] = [
            normed,
            attended,
            d_branch[layer].reshape(ROWS, WIDTH),
            *more[: 2 * layer],
            states[layer + 1],
            tally.reshape(ROWS, 128),
        ]
        gain_sums[layer] = d_norm_m
    *stored, given_1, gain_1, d_qkv_1, d_gains_1 = more
    results[1].insert(1, d_qkv_1)
    attn_grad, given_0, total, in_came, down_came, act_came, tally_came, given_came, *grads_0 = tail(
        inputs,
        dmid,
        gains,
        d_branch[0],
        kept[0][1],
        layout,
        (gain_sums[0], gain_1, gain_sums[1], d_gains_1),
        weights_of[0],
        results,
        given_1,
        (*stored, kept[0][4]),
    )
    (d_gate, d_up, d_down, acts, givens, d_query, d_key, d_value, d_out, *d_gains) = write_outputs(
        attn_grad,
        total,
        grads_0[0],
        results[1][4],
        in_came,
        grads_0[1],
        results[1][5],
        down_came,
        states[1],
        states[2],
        act_came,
        given_0.reshape(ROWS, WIDTH),
        given_1.reshape(ROWS, WIDTH),
        given_came.reshape(ROWS, WIDTH),
    )
    tally = jnp.where(first, results[0][4], results[1][7])
    tally = jnp.where(first, jnp.stack([tally, tally_came]), jnp.stack([tally_came, tally]))
    tally = tally.astype(F32)[:, :, :EXPERTS]
    d_gates = jnp.sum(jnp.where(named, tally[:, :, None, :], 0.0), axis=3)
    return (
        acts[None],
        givens[None],
        *d_gains,
        d_query[None],
        d_key[None],
        d_value[None],
        d_out[None],
        *(grad.reshape(1, 2, 192, WIDTH) for grad in (d_gate, d_up, d_down)),
        d_gates[None],
    )


def solution(mesh):
    placed = (
        P(None, "expert", None),
        P(None, "expert", None),
        P(None, "expert", None),
        P("pipe", None, "expert", None),
        P("pipe", None, "expert", None),
        P("pipe", None),
        P("pipe", None),
        P("pipe", None),
        P("pipe", None),
        P("pipe", "expert", "tensor"),
        P("pipe", "expert", "tensor"),
        P("pipe", "expert", "tensor"),
        P("pipe", "tensor", "expert"),
        P("pipe", "expert", "tensor", None),
        P("pipe", "expert", "tensor", None),
        P("pipe", "expert", "tensor", None),
    )
    return jax.shard_map(
        body,
        mesh=mesh,
        in_specs=placed,
        out_specs=(
            P("pipe", None, "expert", None),
            P("pipe", None, "expert", None),
            P("pipe", None),
            P("pipe", None),
            P("pipe", None),
            P("pipe", None),
            P("pipe", "expert", "tensor"),
            P("pipe", "expert", "tensor"),
            P("pipe", "expert", "tensor"),
            P("pipe", "tensor", "expert"),
            P("pipe", "expert", "tensor", None),
            P("pipe", "expert", "tensor", None),
            P("pipe", "expert", "tensor", None),
            P("pipe", None, "expert", None),
        ),
        check_vma=False,
    )
```

time: 2470 us -> 608 us (0.25)
  waiting for transfers between devices: 1050 us -> 0.01 us
  blocking collectives: 727 us -> 0 us
  Pallas kernels: 0 us -> 594 us
  local copies, waits for them, and re-layouts: 249 us -> 1.46 us
  matrix products: 228 us -> 0 us
  other arithmetic: 135 us -> 3.74 us
  starting transfers between devices: 49.4 us -> 0.68 us
    all_to_all x8 -> x0, waiting for transfers between devices: 629 us -> none  [the longest x6 484 us: return_rows(): lax.all_to_all(block_parts, 'expert', split_axis=0, concat_axis=0, tiled=...]
    pallas_call x0 -> x7, Pallas kernels: none -> 594 us  [the longest x6 582 us: call(): pl.pallas_call(kernel, out_shape=shapes, in_specs=[pl.BlockSpec(memory_sp...]
    psum x11 -> x0, waiting for transfers between devices: 374 us -> none  [the longest x3 123 us: layer_forward(): lax.psum(jnp.dot(attended, w_out, preferred_element_type=jnp.float32), 't...]
    psum x2 -> x0, blocking collectives: 353 us -> none  [the longest x1 344 us: body(): lax.psum((attn_gain_sum / tensor_count, moe_gain_sum / tensor_count, q_ga...]
    all_to_all x4 -> x0, blocking collectives: 324 us -> none  [send_rows(): lax.all_to_all(slot_rows, 'expert', split_axis=0, concat_axis=0, tiled=True)]
    dot_general x90 -> x0, matrix products: 228 us -> none  [the longest x3 19.8 us: layer_backward(): jnp.einsum('secd,efd->secf', d_part, w_down, preferred_element_type=jnp.f...]
    gather x12 -> x0, local copies, waits for them, and re-layouts: 142 us -> none  [the longest x3 46.3 us: layer_backward(): d_part = send_rows(slot_table[slot_owner].reshape(arrived.shape))]
    select_n x30 -> x1, other arithmetic: 56.8 us -> 0.77 us  [body(): tally = jnp.where(first, results[0][4], results[1][7])]
  transfers between devices with their start and end apart: 29 -> 3, of which waited for: 22 -> 0; matrix products, arithmetic and copies ran while one was open for 11% -> 0% of each run, Pallas kernels for 0% -> 9%
where the time goes in v1:
time: 608 us; the launch traced here: 601 us
  Pallas kernels  594 us (98%)
    pallas_call x6, Pallas kernels, call(): pl.pallas_call(kernel, out_shape=shapes, in_specs=[pl.BlockSpec(memory_sp...  582 us
  transfers between devices with their start and end apart: 3, of which 0 were waited for; matrix products, arithmetic and copies ran while one was open for 0% of the time, Pallas kernels for 9%

profile of v1, /device:TPU:0, one launch (start us, length us, event | category | flops | bytes accessed | tf_op | source)
XLA Modules:
  0.0 600.7 jit_solution(6755835747249487792)
XLA Ops:
  0.6 0.1 collective-permute-start
  0.7 0.5 collective-permute-start.1
  1.2 0.1 collective-permute-start.2
  1.3 0.7 select_reduce_fusion.1
  2.1 0.1 copy.35
  2.2 0.1 copy.36
  2.3 0.1 pad.6.clone
  2.4 0.7 maximum_maximum_fusion.refs_5_
  3.1 54.6 %shard_map.263 = (bf16[4,4,128,2304]{3,2,1,0:T(8,128)(2,1)}, bf16[4,4,128,2304]{3,2,1,0:T(8,128)(2,1)}, f32[2,4,4,4,32,128]{5,4,3,2,1,0:T(8,128)}, f32[2,8,2048]...) custom-call(s32[2,1,2]{2,1,0:T(1,128)} %refs_0_.1, bf16[128,1024]{1,0:T(8,128)(2,1)} %bitcast.74, ...), custom_call_target="tpu_custom_call" | custom-call | tf_op jit(solution)/shard_map/pallas_call | solution.py:422
  57.7 0.0 collective-permute-done.refs_11_.refs_9_.refs_17_
  57.7 0.0 copy-start
  57.7 0.0 collective-permute-done.1.refs_12_.refs_10_.refs_18_
  57.7 0.0 collective-permute-done.2.refs_13_.refs_11_.refs_19_
  57.7 1.1 copy-done
  58.9 109.6 %shard_map.264 = (bf16[4,4,4,32,2048]{4,3,2,1,0:T(8,128)(2,1)}, f32[32,2048]{1,0:T(8,128)}, bf16[4,4,4,32,768]{4,3,2,1,0:T(8,128)(2,1)}, bf16[4,32,2048]{2,1,0:T...) custom-call(bf16[2,4,32,2048]{3,2,1,0:T(8,128)(2,1)} %bitcast.62, ...), custom_call_target="tpu_custom_call" | custom-call | tf_op jit(solution)/shard_map/pallas_call | solution.py:422
  168.5 113.6 %shard_map.265 = (bf16[4,4,4,32,2048]{4,3,2,1,0:T(8,128)(2,1)}, f32[32,2048]{1,0:T(8,128)}, bf16[4,4,4,32,768]{4,3,2,1,0:T(8,128)(2,1)}, bf16[4,32,2048]{2,1,0:T...) custom-call(bf16[4,32,2048]{2,1,0:T(8,128)(2,1)} %get-tuple-element.83.refs_0_, ...), custom_call_target="tpu_custom_call" | custom-call | tf_op jit(solution)/shard_map/pallas_call | solution.py:422
  282.1 114.3 %shard_map.266 = (f32[32,2048]{1,0:T(8,128)}, bf16[4,32,2048]{2,1,0:T(8,128)(2,1)}, bf16[4,32,128]{2,1,0:T(8,128)(2,1)}, f32[1,2048]{1,0:T(1,128)}, bf16[768,204...) custom-call(bf16[2,4,32,2048]{3,2,1,0:T(8,128)(2,1)} %bitcast.69, f32[32,2048]{1,0:T(8,128)} %get-tuple-element.85.refs_1_, ...), custom_call_target="tpu_custom_call" | custom-call | tf_op jit(solution)/shard_map/pallas_call | solution.py:422
  396.5 124.4 %shard_map.267 = (f32[32,2048]{1,0:T(8,128)}, bf16[4,32,2048]{2,1,0:T(8,128)(2,1)}, bf16[4,32,128]{2,1,0:T(8,128)(2,1)}, f32[1,2048]{1,0:T(1,128)}, bf16[4,4,4,3...) custom-call(bf16[4,32,2048]{2,1,0:T(8,128)(2,1)} %get-tuple-element., ...), custom_call_target="tpu_custom_call" | custom-call | tf_op jit(solution)/shard_map/pallas_call | solution.py:422
  520.9 0.8 broadcast_select_fusion
  521.7 65.7 %shard_map.268 = (f32[128,2304]{1,0:T(8,128)}, bf16[4,32,2048]{2,1,0:T(8,128)(2,1)}, f32[2,40,128]{2,1,0:T(8,128)}, bf16[768,2048]{1,0:T(8,128)(2,1)}, bf16[384,...) custom-call(bf16[2,4,32,2048]{3,2,1,0:T(8,128)(2,1)} %bitcast.63, ...), custom_call_target="tpu_custom_call" | custom-call | tf_op jit(solution)/shard_map/pallas_call | solution.py:422
  587.4 0.8 fusion.1
  588.3 0.1 copy.37
  588.4 0.7 select_reduce_fusion
  589.0 11.4 %shard_map.269 = (f32[384,2048]{1,0:T(8,128)}, f32[384,2048]{1,0:T(8,128)}, f32[384,2048]{1,0:T(8,128)}, f32[2,128,2048]{2,1,0:T(8,128)}, f32[2,128,2048]{2,1,0:...) custom-call(f32[128,2304]{1,0:T(8,128)} %get-tuple-element.115.refs_, ...), custom_call_target="tpu_custom_call" | custom-call | bytes 25165824 | tf_op jit(solution)/shard_map/pallas_call | solution.py:1050
  (6 shorter events, 0.0 us)
Async XLA Ops:
  0.6 57.1 %collective-permute-start = (bf16[2,192,2048]{2,1,0:T(8,128)(2,1)}, bf16[2,192,2048]{2,1,0:T(8,128)(2,1)S(1)}, u32[]{:S(2)}, u32[]{:S(2)}) collective-permute-start(bf16[2,192,2048]{2,1,0:T(8,128)(2,1)} %bitcast.45), channel_id=1, source_target_pairs={{0,64},{64,0},{1,65},{65,1},{2,66},{66,2},{3,67},{67,3},{4,68},{68... | collective-permute-start | bytes 4718600 | tf_op jit(solution)/shard_map/ppermute | solution.py:1792
  0.7 57.0 %collective-permute-start.1 = (bf16[2,192,2048]{2,1,0:T(8,128)(2,1)}, bf16[2,192,2048]{2,1,0:T(8,128)(2,1)}, u32[]{:S(2)}, u32[]{:S(2)}) collective-permute-start(bf16[2,192,2048]{2,1,0:T(8,128)(2,1)} %bitcast.50), channel_id=1, source_target_pairs={{0,64},{64,0},{1,65},{65,1},{2,66},{66,2},{3,67},{67,3},{4,68},{68... | collective-permute-start | bytes 4718600 | tf_op jit(solution)/shard_map/ppermute | solution.py:1792
  1.2 56.5 %collective-permute-start.2 = (bf16[2,192,2048]{2,1,0:T(8,128)(2,1)}, bf16[2,192,2048]{2,1,0:T(8,128)(2,1)}, u32[]{:S(2)}, u32[]{:S(2)}) collective-permute-start(bf16[2,192,2048]{2,1,0:T(8,128)(2,1)} %bitcast.55), channel_id=1, source_target_pairs={{0,64},{64,0},{1,65},{65,1},{2,66},{66,2},{3,67},{67,3},{4,68},{68... | collective-permute-start | bytes 4718600 | tf_op jit(solution)/shard_map/ppermute | solution.py:1792
  57.7 1.1 copy-start
  396.5 124.4 %copy-start.1 = (bf16[4,32,128]{2,1,0:T(8,128)(2,1)S(1)}, bf16[4,32,128]{2,1,0:T(8,128)(2,1)}, u32[]{:S(2)}) copy-start(bf16[4,32,128]{2,1,0:T(8,128)(2,1)} %get-tuple-element.110) | copy-start | bytes 98308
  521.7 66.7 %copy-start.2 = (s32[1,2,128,8]{2,3,1,0:T(8,128)S(1)}, s32[1,2,128,8]{2,3,1,0:T(8,128)}, u32[]{:S(2)}) copy-start(s32[1,2,128,8]{2,3,1,0:T(8,128)} %param.19) | copy-start | bytes 24580

commit v2 on v1

--- a/solution.py
+++ b/solution.py
@@ -843,15 +843,6 @@
 
         lax.fori_loop(0, RING, product, 0)
         start_reduce(subs)
-    for core in range(2):
-
-        @pl.when(place.pipe == core)
-        def _(core=core):
-            for made in owed(1 - core, (6, 7)):
-                made.start()
-            if core == 0:
-                trade.describe(given_1, came_given, sib, 8).start()
-
     for made in loads:
         made.wait()
     fill = weight_grads(
@@ -877,8 +868,10 @@
 
         @pl.when(place.pipe == core)
         def _(core=core):
-            for made in owed(1 - core, (4, 5)):
+            for made in owed(1 - core, range(4, 8)):
                 made.start()
+            if core == 0:
+                trade.describe(given_1, came_given, sib, 8).start()
 
     together([state_step] + steps)
     for (_, tile), buf in zip(TAIL_SUBS, bufs):
@@ -1289,9 +1282,6 @@
     bufs = token_bufs(bufs)
     place = Place()
     net = Net(send, recv)
-    fetched = fetch_experts(place, layer, own_w, other_w, (w_in, w_down), sems)
-    fetched.append(pltpu.make_async_copy(dense.at[layer], spread, sems.at[5]))
-    fetched[-1].start()
     parts = [
         (0, part_all.at[EVERY + (pl.ds(0, QKV),)]),
         (QKV, part_all.at[EVERY + (pl.ds(QKV, WIDTH - QKV),)]),
@@ -1312,6 +1302,9 @@
 
     else:
         greet(around(place, "xyz"), attend)
+    fetched = fetch_experts(place, layer, own_w, other_w, (w_in, w_down), sems)
+    fetched.append(pltpu.make_async_copy(dense.at[layer], spread, sems.at[5]))
+    fetched[-1].start()
     attn_saved = [
         pltpu.make_async_copy(src, dst, attn_sems.at[3 + i])
         for i, (src, dst) in enumerate(zip(attn_v, results))
@@ -1346,7 +1339,7 @@
         pltpu.make_async_copy(kept_v, kept, sems.at[4]),
     ]
 
-    mixed = []
+    finished = []
 
     def mix(stream):
         def tile(i, _):
@@ -1359,10 +1352,6 @@
             return 0
 
         lax.fori_loop(0, 16, tile, 0)
-        mixed.append(stream)
-        if len(mixed) == 2:
-            for made in saved:
-                made.start()
 
     def down(chunk, stream, by):
         rs, cs = TILES[chunk, stream].at()
@@ -1373,6 +1362,10 @@
     def finish(stream):
         rs = pl.ds(stream * 16, 16)
         held[t, rs, :] = (middle[rs, :] + token_sums(bufs, stream)).astype(BF)
+        finished.append(stream)
+        if len(finished) == 1:
+            for made in saved:
+                made.start()
 
     steps = {
         i: stream_steps(
@@ -1503,15 +1496,10 @@
     place = Place()
     net = Net(send, recv)
     z, x, t = place.at["z"], place.at["x"], place.at["y"]
-    fetched = fetch_experts(place, layer, own_w, other_w, (w_in, w_down), sems)
     d_gain[...] = jnp.zeros((1, WIDTH), F32)
     if layer == 0:
         d_gain_next[...] = jnp.zeros((1, WIDTH), F32)
-    mixed = []
-    for src, dst, i in ((kept, both, 3), (dense.at[layer], spread, 7)):
-        made = pltpu.make_async_copy(src, dst, sems.at[i])
-        made.start()
-        fetched.append(made)
+    mixed, finished = [], []
     attend = None
     if layer == 0:
         w_out = part_all.at[EVERY + (pl.ds(0, 1024),)]
@@ -1534,9 +1522,13 @@
             )
 
     greet(around(place, "xyz"), attend)
+    fetched = fetch_experts(place, layer, own_w, other_w, (w_in, w_down), sems)
+    for src, dst, i in ((kept, both, 3), (dense.at[layer], spread, 7)):
+        made = pltpu.make_async_copy(src, dst, sems.at[i])
+        made.start()
+        fetched.append(made)
     if layer == 1:
         token_copy = pltpu.make_async_copy(tokens, x_all, sems.at[4])
-        token_copy.start()
     else:
         saving = pltpu.make_async_copy(d_qkv_v, d_qkv_out, attn_sems.at[2])
         saving.start()
@@ -1602,8 +1594,8 @@
         mixed.append(stream)
         if layer == 0 and len(mixed) == 2:
             given_out[...] = g_all[z, x]
-            for made in stores:
-                made.start()
+        if layer == 1 and len(mixed) == 1:
+            token_copy.start()
 
     def back_rows(chunk, stream, by):
         rs, cs = TILES[chunk, stream].at()
@@ -1631,6 +1623,10 @@
         dmid[rs, :] = value
         held[t, rs, :] = value.astype(BF)
         add_rows(d_gain, rows)
+        finished.append(stream)
+        if layer == 0 and len(finished) == 1:
+            for made in stores:
+                made.start()
 
     steps = {
         i: stream_steps(

time: 608 us -> 605 us (level)
  no operation moved by 1% of the time
where the time goes in v2:
time: 605 us; the launch traced here: 599 us
  Pallas kernels  592 us (98%)
    pallas_call x6, Pallas kernels, call(): pl.pallas_call(kernel, out_shape=shapes, in_specs=[pl.BlockSpec(memory_sp...  580 us
  transfers between devices with their start and end apart: 3, of which 0 were waited for; matrix products, arithmetic and copies ran while one was open for 0% of the time, Pallas kernels for 9%

profile of v2, /device:TPU:0, one launch (start us, length us, event | category | flops | bytes accessed | tf_op | source)
XLA Modules:
  0.0 598.8 jit_solution(2719140921888137339)
XLA Ops:
  0.6 0.1 collective-permute-start
  0.7 0.5 collective-permute-start.1
  1.2 0.1 collective-permute-start.2
  1.3 0.7 select_reduce_fusion.1
  2.1 0.1 copy.35
  2.2 0.1 copy.36
  2.3 0.1 pad.6.clone
  2.4 0.7 maximum_maximum_fusion.refs_5_
  3.1 54.6 %shard_map.263 = (bf16[4,4,128,2304]{3,2,1,0:T(8,128)(2,1)}, bf16[4,4,128,2304]{3,2,1,0:T(8,128)(2,1)}, f32[2,4,4,4,32,128]{5,4,3,2,1,0:T(8,128)}, f32[2,8,2048]...) custom-call(s32[2,1,2]{2,1,0:T(1,128)} %refs_0_.1, bf16[128,1024]{1,0:T(8,128)(2,1)} %bitcast.74, ...), custom_call_target="tpu_custom_call" | custom-call | tf_op jit(solution)/shard_map/pallas_call | solution.py:422
  57.7 0.0 collective-permute-done.refs_11_.refs_9_.refs_17_
  57.7 0.0 copy-start
  57.7 0.0 collective-permute-done.1.refs_12_.refs_10_.refs_18_
  57.7 0.0 collective-permute-done.2.refs_13_.refs_11_.refs_19_
  57.7 1.1 copy-done
  58.9 110.1 %shard_map.264 = (bf16[4,4,4,32,2048]{4,3,2,1,0:T(8,128)(2,1)}, f32[32,2048]{1,0:T(8,128)}, bf16[4,4,4,32,768]{4,3,2,1,0:T(8,128)(2,1)}, bf16[4,32,2048]{2,1,0:T...) custom-call(bf16[2,4,32,2048]{3,2,1,0:T(8,128)(2,1)} %bitcast.62, ...), custom_call_target="tpu_custom_call" | custom-call | tf_op jit(solution)/shard_map/pallas_call | solution.py:422
  169.0 111.4 %shard_map.265 = (bf16[4,4,4,32,2048]{4,3,2,1,0:T(8,128)(2,1)}, f32[32,2048]{1,0:T(8,128)}, bf16[4,4,4,32,768]{4,3,2,1,0:T(8,128)(2,1)}, bf16[4,32,2048]{2,1,0:T...) custom-call(bf16[4,32,2048]{2,1,0:T(8,128)(2,1)} %get-tuple-element.83.refs_0_, ...), custom_call_target="tpu_custom_call" | custom-call | tf_op jit(solution)/shard_map/pallas_call | solution.py:422
  280.4 113.5 %shard_map.266 = (f32[32,2048]{1,0:T(8,128)}, bf16[4,32,2048]{2,1,0:T(8,128)(2,1)}, bf16[4,32,128]{2,1,0:T(8,128)(2,1)}, f32[1,2048]{1,0:T(1,128)}, bf16[768,204...) custom-call(bf16[2,4,32,2048]{3,2,1,0:T(8,128)(2,1)} %bitcast.69, f32[32,2048]{1,0:T(8,128)} %get-tuple-element.85.refs_1_, ...), custom_call_target="tpu_custom_call" | custom-call | tf_op jit(solution)/shard_map/pallas_call | solution.py:422
  393.9 125.9 %shard_map.267 = (f32[32,2048]{1,0:T(8,128)}, bf16[4,32,2048]{2,1,0:T(8,128)(2,1)}, bf16[4,32,128]{2,1,0:T(8,128)(2,1)}, f32[1,2048]{1,0:T(1,128)}, bf16[4,4,4,3...) custom-call(bf16[4,32,2048]{2,1,0:T(8,128)(2,1)} %get-tuple-element., ...), custom_call_target="tpu_custom_call" | custom-call | tf_op jit(solution)/shard_map/pallas_call | solution.py:422
  519.8 0.8 broadcast_select_fusion
  520.6 65.0 %shard_map.268 = (f32[128,2304]{1,0:T(8,128)}, bf16[4,32,2048]{2,1,0:T(8,128)(2,1)}, f32[2,40,128]{2,1,0:T(8,128)}, bf16[768,2048]{1,0:T(8,128)(2,1)}, bf16[384,...) custom-call(bf16[2,4,32,2048]{3,2,1,0:T(8,128)(2,1)} %bitcast.63, ...), custom_call_target="tpu_custom_call" | custom-call | tf_op jit(solution)/shard_map/pallas_call | solution.py:422
  585.5 0.8 fusion.1
  586.4 0.1 copy.37
  586.4 0.7 select_reduce_fusion
  587.1 11.4 %shard_map.269 = (f32[384,2048]{1,0:T(8,128)}, f32[384,2048]{1,0:T(8,128)}, f32[384,2048]{1,0:T(8,128)}, f32[2,128,2048]{2,1,0:T(8,128)}, f32[2,128,2048]{2,1,0:...) custom-call(f32[128,2304]{1,0:T(8,128)} %get-tuple-element.115.refs_, ...), custom_call_target="tpu_custom_call" | custom-call | bytes 25165824 | tf_op jit(solution)/shard_map/pallas_call | solution.py:1043
  (6 shorter events, 0.0 us)
Async XLA Ops:
  0.6 57.1 %collective-permute-start = (bf16[2,192,2048]{2,1,0:T(8,128)(2,1)}, bf16[2,192,2048]{2,1,0:T(8,128)(2,1)S(1)}, u32[]{:S(2)}, u32[]{:S(2)}) collective-permute-start(bf16[2,192,2048]{2,1,0:T(8,128)(2,1)} %bitcast.45), channel_id=1, source_target_pairs={{0,64},{64,0},{1,65},{65,1},{2,66},{66,2},{3,67},{67,3},{4,68},{68... | collective-permute-start | bytes 4718600 | tf_op jit(solution)/shard_map/ppermute | solution.py:1788
  0.7 57.0 %collective-permute-start.1 = (bf16[2,192,2048]{2,1,0:T(8,128)(2,1)}, bf16[2,192,2048]{2,1,0:T(8,128)(2,1)}, u32[]{:S(2)}, u32[]{:S(2)}) collective-permute-start(bf16[2,192,2048]{2,1,0:T(8,128)(2,1)} %bitcast.50), channel_id=1, source_target_pairs={{0,64},{64,0},{1,65},{65,1},{2,66},{66,2},{3,67},{67,3},{4,68},{68... | collective-permute-start | bytes 4718600 | tf_op jit(solution)/shard_map/ppermute | solution.py:1788
  1.2 56.5 %collective-permute-start.2 = (bf16[2,192,2048]{2,1,0:T(8,128)(2,1)}, bf16[2,192,2048]{2,1,0:T(8,128)(2,1)}, u32[]{:S(2)}, u32[]{:S(2)}) collective-permute-start(bf16[2,192,2048]{2,1,0:T(8,128)(2,1)} %bitcast.55), channel_id=1, source_target_pairs={{0,64},{64,0},{1,65},{65,1},{2,66},{66,2},{3,67},{67,3},{4,68},{68... | collective-permute-start | bytes 4718600 | tf_op jit(solution)/shard_map/ppermute | solution.py:1788
  57.7 1.1 copy-start
  393.9 125.9 %copy-start.1 = (bf16[4,32,128]{2,1,0:T(8,128)(2,1)S(1)}, bf16[4,32,128]{2,1,0:T(8,128)(2,1)}, u32[]{:S(2)}) copy-start(bf16[4,32,128]{2,1,0:T(8,128)(2,1)} %get-tuple-element.110) | copy-start | bytes 98308
  520.5 65.9 %copy-start.2 = (s32[1,2,128,8]{2,3,1,0:T(8,128)S(1)}, s32[1,2,128,8]{2,3,1,0:T(8,128)}, u32[]{:S(2)}) copy-start(s32[1,2,128,8]{2,3,1,0:T(8,128)} %param.19) | copy-start | bytes 24580
